TPU v7x, 256 devices: a whole 4x4x8 slice. The times are simulated.
256 devices in a mesh: long: 16 (over y, x_hi, core), inner: 16 (over x_lo, z).
Axes of the slice: x: 4 (x_hi: 2, x_lo: 2; x = x_hi * 2 + x_lo), y: 4, z: 8, core: 2. Of those that a mesh axis runs over, the one named last changes fastest.
Arguments:
- image_raw: bfloat16 [16384, 1280], P(('long', 'inner')), may hold values from -1 to 1, as said below
- text_raw: bfloat16 [16384, 1280], P(('long', 'inner')), may hold values from -1 to 1, as said below
- log_scale: float32 [1], replicated, may hold values from 4 to 4.6
Outputs:
- grad_image: bfloat16 [16384, 1280], P(('long', 'inner'))
- grad_text: bfloat16 [16384, 1280], P(('long', 'inner'))
- loss: float32 [1], replicated
- grad_log_scale: float32 [1], replicated
Inputs may be any that keep to these rules, and one draw needn't show every extreme that they name: `image_raw`: each image row and its paired text row are partly aligned. `text_raw`: each text row and its paired image row are partly aligned.
All inputs are finite; a program needn't handle non-finite values.
Results may differ from a plain program's by a relative error of at most 0.017.
Values may be sent and summed in bfloat16 or wider, within the bound.
No kernel may reach another device: no remote copies, remote signals or barrier semaphores. Data moves between devices by JAX's collectives and lax.ppermute only.
A program may use at most 64 MiB of HBM per device.

v0:
```python
import itertools

import jax
import jax.numpy as jnp
from jax import lax
from jax.experimental import pallas as pl
from jax.experimental.pallas import tpu as pltpu
from jax.sharding import Mesh, PartitionSpec as P

NORM_EPS = 1e-06
LOG2_E = 1.4426950408889634
AXES = ("y", "xh", "c", "xl", "z")
SIZES = (4, 2, 2, 2, 8)
GROUP = 16
ROWS = 64
VMEM_LIMIT = 24 * 1024 * 1024
F32 = jnp.float32
BF16 = jnp.bfloat16
VMEM = pl.BlockSpec(memory_space=pltpu.VMEM)
SMEM = pl.BlockSpec(memory_space=pltpu.SMEM)


def call(kernel, out, ins, name, flops=0, **more):
    return pl.pallas_call(
        kernel,
        out_shape=out,
        in_specs=ins,
        compiler_params=pltpu.CompilerParams(vmem_limit_bytes=VMEM_LIMIT),
        cost_estimate=pl.CostEstimate(flops=flops, bytes_accessed=1 << 20, transcendentals=0),
        name=name,
        **more,
    )


def shape(*dims, dtype=BF16):
    return jax.ShapeDtypeStruct(dims, dtype)


def permute(array, move):
    flat = lambda x, y, z, c: (((y * 2 + x // 2) * 2 + c) * 2 + x % 2) * 8 + z
    pairs = []
    for y, xh, c, xl, z in itertools.product(*map(range, SIZES)):
        x2, y2, z2, c2 = move(2 * xh + xl, y, z, c)
        pairs.append((flat(2 * xh + xl, y, z, c), flat(x2 % 4, y2 % 4, z2 % 8, c2 % 2)))
    return lax.ppermute(array, AXES, pairs)


def to_sibling(array):
    return permute(array, lambda x, y, z, c: (x, y, z, 1 - c))


def along(array, axis, step):
    steps = {"x": (step, 0, 0), "y": (0, step, 0), "z": (0, 0, step)}[axis]
    return permute(array, lambda x, y, z, c: (x + steps[0], y + steps[1], z + steps[2], c))


def first_axis(array, step):
    return permute(array, lambda x, y, z, c: (x + step, y, z, c) if c == 0 else (x, y + step, z, c))


def second_axis(array, step):
    return permute(array, lambda x, y, z, c: (x, y + step, z, c) if c == 0 else (x + step, y, z, c))


def ring(array, step):
    return permute(array, lambda x, y, z, c: (x, y, z + (step if c == 0 else -step), c))


def unit_rows(ref):
    values = ref[...].astype(F32)
    recip = 1.0 / jnp.sqrt(jnp.sum(values * values, axis=1, keepdims=True) + NORM_EPS)
    return values * recip, recip


def normalize_kernel(raw_ref, hat_ref):
    hat_ref[...] = unit_rows(raw_ref)[0].astype(BF16)


def diagonal_kernel(img_hat_ref, txt_hat_ref, diag_ref):
    products = img_hat_ref[...].astype(F32) * txt_hat_ref[...].astype(F32)
    diag_ref[...] = jnp.full(diag_ref.shape, jnp.sum(products), F32)


def encode(ref, at, scalars):
    high = scalars.astype(BF16).astype(F32)
    middle = (scalars - high).astype(BF16).astype(F32)
    parts = (high, middle, scalars - high - middle)
    row = lax.broadcasted_iota(jnp.int32, (16, 128), 0)
    block = jnp.zeros((16, 128), F32)
    for k, part in enumerate(parts):
        block = jnp.where(row == k, jnp.concatenate([part, part], axis=0), block)
    ref[at : at + 16, 0:128] = block.astype(BF16)
    ref[at : at + 16, 128:] = jnp.zeros((16, ref.shape[1] - 128), BF16)


def decode(ref, at):
    block = ref[at : at + 16, 0:128].astype(F32)
    return jnp.broadcast_to(jnp.sum(block, axis=0, keepdims=True), (8, 128))


def pair_kernel(core_ref, keep_ref, arrived_ref, far_ref, rest_ref, own_ref, scalar_ref):
    total = keep_ref[0:512, :].astype(F32) + arrived_ref[0:512, :].astype(F32)
    total = total.astype(BF16)
    rest_ref[...] = total[0:384]
    far_ref[0:64, :] = total[384:448]
    own_ref[...] = total[448:512]
    scalars = decode(keep_ref, 512) + decode(arrived_ref, 512)
    scalar_ref[...] = scalars
    encode(far_ref, 64, jnp.where(core_ref[0] == 0, scalars, 0.0))


def ring_fold_kernel(start, base_ref, arrived_ref, scalar_ref, out_ref):
    rows = arrived_ref.shape[0] - 16
    out_ref[0:rows, :] = (
        base_ref[start : start + rows, :].astype(F32) + arrived_ref[0:rows, :].astype(F32)
    ).astype(BF16)
    if rows < 128:
        out_ref[rows:128, :] = base_ref[start + rows : start + 128, :]
    encode(out_ref, 128, scalar_ref[...] + decode(arrived_ref, rows))


def last_fold_kernel(base_ref, arrived_ref, scalar_ref, own_ref, sib_ref):
    for k, out in enumerate((own_ref, sib_ref)):
        cut = slice(k * 64, (k + 1) * 64)
        out[0:64, :] = (base_ref[cut, :].astype(F32) + arrived_ref[cut, :].astype(F32)).astype(BF16)
    encode(sib_ref, 64, scalar_ref[...] + decode(arrived_ref, 128))


def plane_fold_kernel(minus_ref, plus_ref, low_ref, high_ref, scalar_ref, to_minus_ref, to_plus_ref):
    to_minus_ref[0:128, :] = (minus_ref[0:128, :].astype(F32) + low_ref[0:128, :].astype(F32)).astype(BF16)
    to_minus_ref[128:256, :] = minus_ref[128:256, :]
    to_plus_ref[0:128, :] = plus_ref[0:128, :]
    to_plus_ref[128:256, :] = (plus_ref[128:256, :].astype(F32) + high_ref[...].astype(F32)).astype(BF16)
    encode(to_minus_ref, 256, scalar_ref[...] + decode(low_ref, 128))
    encode(to_plus_ref, 256, scalar_ref[...])


def line_kernel(own_ref, down_ref, up_ref, scalar_ref, *outs):
    scalars = scalar_ref[...] + decode(down_ref, 256) + decode(up_ref, 256)
    for k, out in enumerate(outs[:4]):
        cut = slice(k * 64, (k + 1) * 64)
        out[0:64, :] = (
            own_ref[cut, :].astype(F32) + down_ref[cut, :].astype(F32) + up_ref[cut, :].astype(F32)
        ).astype(BF16)
        if k:
            encode(out, 64, scalars)
    outs[4][...] = scalars


def copy_rows(source, first, target, at, rows):
    @pl.loop(0, rows // 32)
    def _(k):
        cut = pl.ds(pl.multiple_of(first + k * 32, 32), 32)
        target[pl.ds(pl.multiple_of(at + k * 32, 32), 32), :] = source[cut, :]


def logits_kernel(img_order, txt_order, *refs):
    row_place, col_place, scale_ref, diag_ref = refs[:4]
    n_img, n_txt = 9, 5
    img_refs, txt_refs = refs[4 : 4 + n_img], refs[4 + n_img : 4 + n_img + n_txt]
    img_all, txt_all, logit_ref, row_ref, col_ref = refs[4 + n_img + n_txt :]
    tile = 256
    for blocks, order, target in ((img_refs, img_order, img_all), (txt_refs, txt_order, txt_all)):
        at = 0
        for k, first, size in order:
            copy_rows(blocks[k], first, target, at, size)
            at += size
    row_sums, row_slopes = [], []
    for step in range(4):
        cut = slice(step * tile, (step + 1) * tile)
        logits = lax.dot_general(
            img_all[...], txt_all[cut, :], (((1,), (1,)), ((), ())), preferred_element_type=F32
        )
        logit_ref[:, cut] = logits
        powers = jnp.exp2(logits * scale_ref[2] - scale_ref[3])
        weighted = powers * logits
        row_sums.append(powers[:, 0:128] + powers[:, 128:256])
        row_slopes.append(weighted[:, 0:128] + weighted[:, 128:256])
        sums = jnp.sum(powers, axis=0, keepdims=True)
        slopes = jnp.sum(weighted, axis=0, keepdims=True)
        for k in range(tile // 64):
            at = col_place[step * (tile // 64) + k]
            part = slice(k * 64, (k + 1) * 64)
            col_ref[pl.ds(at, 1), :] = jnp.concatenate([sums[:, part], slopes[:, part]], axis=1)
    sums = jnp.sum(sum(row_sums).T, axis=0, keepdims=True)
    slopes = jnp.sum(sum(row_slopes).T, axis=0, keepdims=True)
    for k in range(GROUP):
        part = slice(k * 64, (k + 1) * 64)
        row_ref[pl.ds(row_place[k], 1), :] = jnp.concatenate([sums[:, part], slopes[:, part]], axis=1)
    row_ref[16:24, :] = diag_ref[...]


def grad_img_tiles(half, scale_ref, logit_ref, txt_ref, row_half, col_half, grad_ref, dlogit_ref):
    rows = slice(half * 512, (half + 1) * 512)
    powers = jnp.exp2(logit_ref[rows, :] * scale_ref[2] - scale_ref[3])
    by_row = jnp.concatenate([row_half[rows, :]] * 8, axis=1)
    dlogit_ref[...] = (powers * (by_row + col_half[0:1, :])).astype(BF16)

    @pl.loop(0, 5)
    def _(step):
        cut = pl.ds(pl.multiple_of(step * 256, 256), 256)
        grad = jnp.dot(dlogit_ref[...], txt_ref[:, cut], preferred_element_type=F32)
        grad_ref[0:512, cut] = grad.astype(BF16)


def grad_img_kernel(*refs):
    row_place, col_place, scale_ref, logit_ref, txt_ref = refs[:5]
    rows_in, cols_in = refs[5:8], refs[8:12]
    grad_ref, dlogit_ref, row_half, col_half, row_scalars, col_scalars = refs[12:-2]
    row_sum, col_sum = refs[-2:]
    row_sum[...] = rows_in[0][...] + rows_in[1][...] + rows_in[2][...]
    col_sum[...] = cols_in[0][...] + cols_in[1][...] + cols_in[2][...] + cols_in[3][...]
    row = jnp.concatenate([row_sum[pl.ds(row_place[k], 1), 0:64] for k in range(16)], axis=1)
    col = jnp.concatenate([col_sum[pl.ds(col_place[k], 1), 0:64] for k in range(16)], axis=1)
    row_half[...] = jnp.broadcast_to(0.5 / row, (128, 1024)).T
    col_half[...] = jnp.broadcast_to(0.5 / col, (8, 1024))
    lane = lax.broadcasted_iota(jnp.int32, (8, 128), 1)

    def scalars(sums, last):
        log_sum = jnp.sum(jnp.log(sums[0:16, 0:64]))
        slope = 0.5 * jnp.sum(sums[0:16, 64:128] / sums[0:16, 0:64])
        return jnp.where(lane == 0, log_sum, jnp.where(lane == 1, slope, last))

    row_scalars[...] = scalars(row_sum, row_sum[16:24, :])
    col_scalars[...] = scalars(col_sum, 0.0)
    encode(grad_ref, 512, col_scalars[...])
    grad_img_tiles(0, scale_ref, logit_ref, txt_ref, row_half, col_half, grad_ref, dlogit_ref)


def grad_img_rest_kernel(scale_ref, logit_ref, txt_ref, row_half, col_half, scalar_ref, grad_ref, dlogit_ref):
    encode(grad_ref, 512, scalar_ref[...])
    grad_img_tiles(1, scale_ref, logit_ref, txt_ref, row_half, col_half, grad_ref, dlogit_ref)


def grad_txt_tile(start, low_ref, high_ref, img_ref):
    return sum(
        lax.dot_general(
            part[:, pl.ds(start, 256)],
            img_ref[k * 512 : (k + 1) * 512, :],
            (((0,), (0,)), ((), ())),
            preferred_element_type=F32,
        )
        for k, part in enumerate((low_ref, high_ref))
    ).astype(BF16)


def grad_txt_far_kernel(low_ref, high_ref, img_ref, scalar_ref, far_low_ref, far_high_ref):
    grad = grad_txt_tile(768, low_ref, high_ref, img_ref)
    far_low_ref[0:128, :] = grad[0:128]
    far_high_ref[...] = grad[128:256]
    encode(far_low_ref, 128, scalar_ref[...])


def grad_txt_kernel(low_ref, high_ref, img_ref, *outs):
    step = pl.program_id(0)
    grad = grad_txt_tile(pl.multiple_of(step * 256, 256), low_ref, high_ref, img_ref)
    for k, ref in enumerate(outs):

        @pl.when(step == k)
        def _():
            ref[...] = grad


def finish_kernel(scale_ref, img_ref, txt_ref, img_hat_ref, txt_hat_ref, *refs):
    own_img, ring_img, sib_img, for_sib, own_txt, txt1, txt2, txt3, col_ref, row_ref = refs[:10]
    grad_img_ref, grad_txt_ref, loss_ref, slope_ref = refs[10:]
    scale = scale_ref[0]
    for raw, other, parts, out in (
        (img_ref, txt_hat_ref, (own_img, ring_img, sib_img), grad_img_ref),
        (txt_ref, img_hat_ref, (own_txt, txt1, txt2, txt3), grad_txt_ref),
    ):
        unit, recip = unit_rows(raw)
        total = sum(part[0:64, :].astype(F32) for part in parts)
        grad_hat = scale * (total - other[...].astype(F32))
        inner = jnp.sum(grad_hat * unit, axis=1, keepdims=True)
        out[...] = (recip * (grad_hat - unit * inner)).astype(BF16)
    cols = col_ref[...] + decode(for_sib, 64) + decode(sib_img, 64)
    rows = row_ref[...] + decode(txt1, 64) + decode(txt2, 64) + decode(txt3, 64)
    batch = ROWS * GROUP * GROUP
    diag_sum = scale * rows[0, 2]
    logs = cols[0, 0] + rows[0, 0] + 2.0 * batch * scale_ref[1]
    loss_ref[0] = (logs - 2.0 * diag_sum) / (2 * batch)
    slope_ref[0] = (scale * (cols[0, 1] + rows[0, 1]) - diag_sum) / batch


def places():
    y, z, core = lax.axis_index("y"), lax.axis_index("z"), lax.axis_index("c")
    x = 2 * lax.axis_index("xh") + lax.axis_index("xl")
    near = jnp.array([0, 3, 1, 2], jnp.int32)
    first, second = jnp.tile(near, 4), jnp.repeat(near, 4)
    on_x = jnp.where(core == 0, first, second)
    on_y = jnp.where(core == 0, second, first)
    cols = ((y + on_y) % 4) * 4 + (x + on_x) % 4
    distance = jnp.array([-1, -1, -2, -2, -3, -3, -4, 0, 1, 1, 2, 2, 3, 3, 4, 0], jnp.int32)
    others = jnp.array([1, 0, 1, 0, 1, 0, 1, 1, 0, 1, 0, 1, 0, 1, 0, 0], jnp.int32)
    way = jnp.where(core == 0, -1, 1)
    rows = ((core + others) % 2) * 8 + (z + way * distance) % 8
    return rows.astype(jnp.int32), cols.astype(jnp.int32)


def per_device(image_raw, text_raw, log_scale):
    rows, width = image_raw.shape
    total = rows * GROUP
    img_hat = call(normalize_kernel, shape(rows, width), [VMEM], "normalize_img")(image_raw)
    txt_hat = call(normalize_kernel, shape(rows, width), [VMEM], "normalize_txt")(text_raw)
    diag = call(diagonal_kernel, shape(8, 128, dtype=F32), [VMEM] * 2, "diagonal")(img_hat, txt_hat)

    scale = jnp.exp(log_scale[0])
    shift = jnp.maximum(1.01 * scale - 70.0, 0.0)
    scales = jnp.stack([scale, shift, scale * LOG2_E, shift * LOG2_E])
    row_place, col_place = places()

    sib = to_sibling(img_hat)
    below, above, far = first_axis(txt_hat, 1), first_axis(txt_hat, -1), first_axis(txt_hat, 2)
    ring1 = ring(jnp.concatenate([img_hat, sib], axis=0), 1)
    line = jnp.concatenate([txt_hat, below, above, far], axis=0)
    up, down = second_axis(line, 1), second_axis(line, -1)
    ring1, _ = lax.optimization_barrier((ring1, line))
    ring2 = ring(ring1, 1)
    low_far, high_far = second_axis(up[:128], 1), second_axis(down[128:], -1)
    ring3 = ring(ring2, 1)
    ring3, _, _ = lax.optimization_barrier((ring3, up, down))
    ring4 = ring(ring3, 1)
    img_blocks = [to_sibling(block) for block in (ring1, ring2, ring3)] + [sib, ring1, ring2, ring3, ring4, img_hat]
    img_order = [(0, 0, 128), (1, 0, 128), (2, 0, 128), (7, 64, 64), (3, 0, 64)]
    img_order += [(4, 0, 128), (5, 0, 128), (6, 0, 128), (7, 0, 64), (8, 0, 64)]
    txt_blocks = [line, up, down, low_far, high_far]
    txt_order = [(k, 0, block.shape[0]) for k, block in enumerate(txt_blocks)]

    flops = 2 * total * total * width
    img_all, txt_all, logits, row_part, col_part = call(
        lambda *refs: logits_kernel(img_order, txt_order, *refs),
        (
            shape(total, width),
            shape(total, width),
            shape(total, total, dtype=F32),
            shape(24, 128, dtype=F32),
            shape(16, 128, dtype=F32),
        ),
        [SMEM] * 3 + [VMEM] * (1 + len(img_blocks) + len(txt_blocks)),
        "logits",
        flops,
    )(row_place, col_place, scales, diag, *img_blocks, *txt_blocks)

    row_pair = row_part + to_sibling(row_part)
    col_line = col_part + along(col_part, "x", 1) + along(col_part, "x", 2) + along(col_part, "x", 3)
    lower, upper = along(row_pair, "z", 1), along(row_pair, "z", -1)
    two = row_pair + lower
    three = two + upper
    row_parts = [three, along(three, "z", 3), along(two, "z", -3)]
    col_parts = [col_line] + [along(col_line, "y", k) for k in (1, 2, 3)]

    eight = shape(8, 128, dtype=F32)
    half_grad = (shape(total // 2 + 16, width), shape(total // 2, total))
    send, dlogits_low, row_half, col_half, row_scalars, col_scalars = call(
        grad_img_kernel,
        half_grad + (shape(total, 128, dtype=F32), shape(8, total, dtype=F32), eight, eight),
        [SMEM] * 3 + [VMEM] * 9,
        "grad_img",
        flops // 2,
        scratch_shapes=[pltpu.VMEM((24, 128), F32), pltpu.VMEM((16, 128), F32)],
    )(row_place, col_place, scales, logits, txt_all, *row_parts, *col_parts)
    arrived = to_sibling(send)
    keep, dlogits_high = call(
        grad_img_rest_kernel,
        half_grad,
        [SMEM] + [VMEM] * 5,
        "grad_img_rest",
        flops // 2,
    )(scales, logits, txt_all, row_half, col_half, col_scalars)
    core = jnp.reshape(lax.axis_index("c"), (1,)).astype(jnp.int32)
    far, rest, own_img, col_scalars = call(
        pair_kernel,
        (shape(80, width), shape(384, width), shape(64, width), shape(8, 128, dtype=F32)),
        [SMEM] + [VMEM] * 2,
        "pair",
    )(core, keep, arrived)
    ring1 = ring(far, -1)
    far_low, far_high = call(
        grad_txt_far_kernel,
        (shape(144, width), shape(128, width)),
        [VMEM] * 4,
        "grad_txt_far",
        flops // 4,
    )(dlogits_low, dlogits_high, img_all, row_scalars)
    low, high = second_axis(far_low, -1), second_axis(far_high, 1)
    txt_own, txt_minus, txt_plus = call(
        grad_txt_kernel,
        (shape(256, width),) * 3,
        [VMEM] * 3,
        "grad_txt",
        flops // 4 * 3,
        grid=(3,),
        out_specs=(VMEM,) * 3,
    )(dlogits_low, dlogits_high, img_all)

    def ring_fold(start, arrived):
        return call(
            lambda *refs: ring_fold_kernel(start, *refs), shape(144, width), [VMEM] * 3, "ring_fold"
        )(rest, arrived, col_scalars)

    ring1, _ = lax.optimization_barrier((ring1, txt_own))
    ring2 = ring(ring_fold(256, ring1), -1)
    to_minus, to_plus = call(
        plane_fold_kernel, (shape(272, width),) * 2, [VMEM] * 5, "plane_fold"
    )(txt_minus, txt_plus, low, high, row_scalars)
    down, up = second_axis(to_minus, -1), second_axis(to_plus, 1)
    ring2, _ = lax.optimization_barrier((ring2, to_plus))
    ring3 = ring(ring_fold(128, ring2), -1)
    own_txt, *sends, row_scalars = call(
        line_kernel,
        (shape(64, width),) + (shape(80, width),) * 3 + (shape(8, 128, dtype=F32),),
        [VMEM] * 4,
        "line",
    )(txt_own, down, up, row_scalars)
    to_own, to_sib = call(
        last_fold_kernel, (shape(64, width), shape(80, width)), [VMEM] * 3, "last_fold"
    )(rest, ring3, col_scalars)
    for_sib = ring(to_sib, -1)
    txt_parts = [own_txt] + [first_axis(part, step) for part, step in zip(sends, (-1, 1, 2))]
    img_parts = [own_img, ring(to_own, -1), to_sibling(for_sib), for_sib]

    scalar = shape(1, dtype=F32)
    return call(
        finish_kernel,
        (shape(rows, width), shape(rows, width), scalar, scalar),
        [SMEM] + [VMEM] * 14,
        "finish",
        out_specs=(VMEM, VMEM, SMEM, SMEM),
    )(scales, image_raw, text_raw, img_hat, txt_hat, *img_parts, *txt_parts, col_scalars, row_scalars)


def solution(mesh):
    mesh = Mesh(mesh.devices.reshape(SIZES), AXES)
    spec = P(AXES, None)
    return jax.shard_map(
        per_device, mesh=mesh, in_specs=(spec, spec, P()), out_specs=(spec, spec, P(), P()), check_vma=False
    )
```

profile of v0, /device:TPU:1, one launch (start us, length us, event | category | flops | bytes accessed | tf_op | source)
XLA Modules:
  0.0 118.0 jit_solution(1751708594481897944)
XLA Ops:
  0.6 0.9 copy-done
  1.5 0.1 normalize_img.1.img_hat_ref.refs_12_
  1.7 3.3 %collective-permute-start = (bf16[64,1280]{1,0:T(8,128)(2,1)S(1)}, bf16[64,1280]{1,0:T(8,128)(2,1)S(1)}, u32[]{:S(2)}, u32[]{:S(2)}) collective-permute-start(bf16[64,1280]{1,0:T(8,128)(2,1)S(1)} %normalize_img.1.img_hat_ref.refs_12_), channel_id=1, source_target_pairs={{0,16},{1,17},{2,18},{3,19},{4,20},{5,21},{6,22},{7,23},{8,24},{9,... | collective-permute-start | bytes 491528 | tf_op jit(solution)/shard_map/ppermute | solution.py:45
  5.0 0.9 copy-done.2
  5.9 0.1 normalize_txt.1.txt_hat_ref
  6.1 1.3 %collective-permute-start.4 = (bf16[64,1280]{1,0:T(8,128)(2,1)S(1)}, bf16[64,1280]{1,0:T(8,128)(2,1)S(1)}, u32[]{:S(2)}, u32[]{:S(2)}) collective-permute-start(bf16[64,1280]{1,0:T(8,128)(2,1)S(1)} %normalize_txt.1.txt_hat_ref), channel_id=1, source_target_pairs={{0,32},{1,33},{2,34},{3,35},{4,36},{5,37},{6,38},{7,39},{8,40},{9,... | collective-permute-start | bytes 491528 | tf_op jit(solution)/shard_map/ppermute | solution.py:45
  7.3 0.8 collective-permute-start.3
  8.1 0.7 collective-permute-start.2
  8.9 5.7 %collective-permute-start.1 = (bf16[128,1280]{1,0:T(8,128)(2,1)S(1)}, bf16[128,1280]{1,0:T(8,128)(2,1)S(1)}, u32[]{:S(2)}, u32[]{:S(2)}) collective-permute-start(bf16[128,1280]{1,0:T(8,128)(2,1)S(1)} %pad_maximum_fusion.1), channel_id=1, source_target_pairs={{0,1},{1,2},{2,3},{3,4},{4,5},{5,6},{6,7},{7,0},{8,9},{9,10},{10,1... | collective-permute-start | bytes 983048 | tf_op jit(solution)/shard_map/ppermute | solution.py:45
  14.6 2.6 %collective-permute-start.10 = (bf16[256,1280]{1,0:T(8,128)(2,1)S(1)}, bf16[256,1280]{1,0:T(8,128)(2,1)S(1)}, u32[]{:S(2)}, u32[]{:S(2)}) collective-permute-start(bf16[256,1280]{1,0:T(8,128)(2,1)S(1)} %pad_maximum_fusion.refs_13_), channel_id=1, source_target_pairs={{0,192},{1,193},{2,194},{3,195},{4,196},{5,197},{6,198},{7,199},{8... | collective-permute-start | bytes 1966088 | tf_op jit(solution)/shard_map/ppermute | solution.py:45
  17.1 1.4 %collective-permute-done.1.refs_8_ = bf16[128,1280]{1,0:T(8,128)(2,1)S(1)} collective-permute-done((bf16[128,1280]{1,0:T(8,128)(2,1)S(1)}, bf16[128,1280]{1,0:T(8,128)(2,1)S(1)}, u32[]{:S(2)}, u32[]{:S(2)}) %collective-permute-start.1) | collective-permute-done | bytes 327712 | tf_op jit(solution)/shard_map/ppermute | solution.py:45
  18.5 3.1 %collective-permute-start.6 = (bf16[128,1280]{1,0:T(8,128)(2,1)S(1)}, bf16[128,1280]{1,0:T(8,128)(2,1)S(1)}, u32[]{:S(2)}, u32[]{:S(2)}) collective-permute-start(bf16[128,1280]{1,0:T(8,128)(2,1)S(1)} %collective-permute-done.1.refs_8_), channel_id=1, source_target_pairs={{0,1},{1,2},{2,3},{3,4},{4,5},{5,6},{6,7},{7,0},{8,9},{9,10},{10,1... | collective-permute-start | bytes 983048 | tf_op jit(solution)/shard_map/ppermute | solution.py:45
  21.7 4.0 %collective-permute-done.6.refs_9_ = bf16[128,1280]{1,0:T(8,128)(2,1)S(1)} collective-permute-done((bf16[128,1280]{1,0:T(8,128)(2,1)S(1)}, bf16[128,1280]{1,0:T(8,128)(2,1)S(1)}, u32[]{:S(2)}, u32[]{:S(2)}) %collective-permute-start.6) | collective-permute-done | bytes 327712 | tf_op jit(solution)/shard_map/ppermute | solution.py:45
  25.7 3.4 %collective-permute-start.8 = (bf16[128,1280]{1,0:T(8,128)(2,1)S(1)}, bf16[128,1280]{1,0:T(8,128)(2,1)S(1)}, u32[]{:S(2)}, u32[]{:S(2)}) collective-permute-start(bf16[128,1280]{1,0:T(8,128)(2,1)S(1)} %collective-permute-done.6.refs_9_), channel_id=1, source_target_pairs={{0,1},{1,2},{2,3},{3,4},{4,5},{5,6},{6,7},{7,0},{8,9},{9,10},{10,1... | collective-permute-start | bytes 983048 | tf_op jit(solution)/shard_map/ppermute | solution.py:45
  29.1 0.1 collective-permute-start.5
  29.2 0.2 diagonal.1.refs_3_
  30.2 0.1 add.91
  30.3 0.1 add.86
  30.4 2.7 %collective-permute-start.14 = (bf16[128,1280]{1,0:T(8,128)(2,1)S(1)}, bf16[128,1280]{1,0:T(8,128)(2,1)S(1)}, u32[]{:S(2)}, u32[]{:S(2)}) collective-permute-start(bf16[128,1280]{1,0:T(8,128)(2,1)S(1)} %slice.9), channel_id=1, source_target_pairs={{0,192},{1,193},{2,194},{3,195},{4,196},{5,197},{6,198},{7,199},{8... | collective-permute-start | bytes 983048 | tf_op jit(solution)/shard_map/ppermute | solution.py:45
  33.1 0.1 collective-permute-start.13
  33.2 0.7 collective-permute-start.7
  33.9 3.0 %collective-permute-start.12 = (bf16[128,1280]{1,0:T(8,128)(2,1)S(1)}, bf16[128,1280]{1,0:T(8,128)(2,1)S(1)}, u32[]{:S(2)}, u32[]{:S(2)}) collective-permute-start(bf16[128,1280]{1,0:T(8,128)(2,1)S(1)} %collective-permute-done.8.refs_10_), channel_id=1, source_target_pairs={{0,1},{1,2},{2,3},{3,4},{4,5},{5,6},{6,7},{7,0},{8,9},{9,10},{10,1... | collective-permute-start | bytes 983048 | tf_op jit(solution)/shard_map/ppermute | solution.py:45
  36.9 0.6 collective-permute-start.11
  37.6 3.0 %collective-permute-done.13.refs_16_ = bf16[128,1280]{1,0:T(8,128)(2,1)S(1)} collective-permute-done((bf16[128,1280]{1,0:T(8,128)(2,1)S(1)}, bf16[128,1280]{1,0:T(8,128)(2,1)S(1)}, u32[]{:S(2)}, u32[]{:S(2)}) %collective-permute-start.13) | collective-permute-done | bytes 327712 | tf_op jit(solution)/shard_map/ppermute | solution.py:45
  40.6 0.3 collective-permute-done.12.refs_11_
  40.9 5.2 %logits.1 = (bf16[1024,1280]{1,0:T(8,128)(2,1)S(1)}, bf16[1024,1280]{1,0:T(8,128)(2,1)S(1)}, f32[1024,1024]{1,0:T(8,128)S(1)}, f32[24,128]{1,0:T(8,128)S(1)}, f32[16,128]{1,0:T(8,128)S(1)}) custom-call(s32[16]{0:T(128)S(1)} %get-tuple-element.78.refs_0_, s32[16]{0:T(128)S(1)} %get-tuple-element.79.refs_1_, f32[4]{0:T(128)S(1)} %pad_maximum_fusion.2.refs_2_.scale_ref, ...), custom_call_target="tpu_custom_call" | custom-call | flops 2684354560 | bytes 1048576 | tf_op jit(solution)/shard_map/logits/pallas_call | solution.py:331
  46.1 4.9 %collective-permute-start.15 = (f32[24,128]{1,0:T(8,128)S(1)}, f32[24,128]{1,0:T(8,128)S(1)}, u32[]{:S(2)}, u32[]{:S(2)}) collective-permute-start(f32[24,128]{1,0:T(8,128)S(1)} %get-tuple-element.43), channel_id=1, source_target_pairs={{0,16},{1,17},{2,18},{3,19},{4,20},{5,21},{6,22},{7,23},{8,24},{9,... | collective-permute-start | bytes 36872 | tf_op jit(solution)/shard_map/ppermute | solution.py:45
  51.0 0.8 collective-permute-done.15
  51.9 1.5 %collective-permute-start.16 = (f32[24,128]{1,0:T(8,128)S(1)}, f32[24,128]{1,0:T(8,128)S(1)}, u32[]{:S(2)}, u32[]{:S(2)}) collective-permute-start(f32[24,128]{1,0:T(8,128)S(1)} %add.94), channel_id=1, source_target_pairs={{0,1},{1,2},{2,3},{3,4},{4,5},{5,6},{6,7},{7,0},{8,9},{9,10},{10,1... | collective-permute-start | bytes 36872 | tf_op jit(solution)/shard_map/ppermute | solution.py:45
  53.3 1.7 %collective-permute-start.22 = (f32[16,128]{1,0:T(8,128)S(1)}, f32[16,128]{1,0:T(8,128)S(1)}, u32[]{:S(2)}, u32[]{:S(2)}) collective-permute-start(f32[16,128]{1,0:T(8,128)S(1)} %get-tuple-element.44), channel_id=1, source_target_pairs={{0,40},{1,41},{2,42},{3,43},{4,44},{5,45},{6,46},{7,47},{8,0},{9,1... | collective-permute-start | bytes 24584 | tf_op jit(solution)/shard_map/ppermute | solution.py:45
  55.1 0.6 collective-permute-start.20
  55.6 3.4 %collective-permute-start.19 = (f32[24,128]{1,0:T(8,128)S(1)}, f32[24,128]{1,0:T(8,128)S(1)}, u32[]{:S(2)}, u32[]{:S(2)}) collective-permute-start(f32[24,128]{1,0:T(8,128)S(1)} %get-tuple-element.75), channel_id=1, source_target_pairs={{0,5},{1,6},{2,7},{3,0},{4,1},{5,2},{6,3},{7,4},{8,13},{9,14},{10,... | collective-permute-start | bytes 36872 | tf_op jit(solution)/shard_map/ppermute | solution.py:45
  59.0 3.0 %collective-permute-start.25 = (f32[16,128]{1,0:T(8,128)S(1)}, f32[16,128]{1,0:T(8,128)S(1)}, u32[]{:S(2)}, u32[]{:S(2)}) collective-permute-start(f32[16,128]{1,0:T(8,128)S(1)} %add_add_fusion.refs_8_), channel_id=1, source_target_pairs={{0,192},{1,193},{2,194},{3,195},{4,196},{5,197},{6,198},{7,199},{8... | collective-permute-start | bytes 24584 | tf_op jit(solution)/shard_map/ppermute | solution.py:45
  62.1 0.1 collective-permute-start.24
  62.2 0.7 collective-permute-start.23
  62.9 3.2 %collective-permute-done.24.refs_10_ = f32[16,128]{1,0:T(8,128)S(1)} collective-permute-done((f32[16,128]{1,0:T(8,128)S(1)}, f32[16,128]{1,0:T(8,128)S(1)}, u32[]{:S(2)}, u32[]{:S(2)}) %collective-permute-start.24) | collective-permute-done | bytes 8224 | tf_op jit(solution)/shard_map/ppermute | solution.py:45
  66.1 3.3 %grad_img.1 = (bf16[528,1280]{1,0:T(8,128)(2,1)S(1)}, bf16[512,1024]{1,0:T(8,128)(2,1)S(1)}, f32[1024,128]{1,0:T(8,128)S(1)}, f32[8,1024]{1,0:T(8,128)S(1)}, f32[8,128]{1,0:T(8,128)S(1)}, /*index=5*/f32[8,128]{1,0:T(8,128)S(1)}) custom-call(s32[16]{0:T(128)S(1)} %get-tuple-element.78.refs_0_, s32[16]{0:T(128)S(1)} %get-tuple-element.79.refs_1_, ...), custom_call_target="tpu_custom_call" | custom-call | flops 1342177280 | bytes 1048576 | tf_op jit(solution)/shard_map/grad_img/pallas_call | solution.py:355
  69.4 4.2 %collective-permute-start.26 = (bf16[528,1280]{1,0:T(8,128)(2,1)S(1)}, bf16[528,1280]{1,0:T(8,128)(2,1)S(1)}, u32[]{:S(2)}, u32[]{:S(2)}) collective-permute-start(bf16[528,1280]{1,0:T(8,128)(2,1)S(1)} %get-tuple-element.49), channel_id=1, source_target_pairs={{0,16},{1,17},{2,18},{3,19},{4,20},{5,21},{6,22},{7,23},{8,24},{9,... | collective-permute-start | bytes 4055048 | tf_op jit(solution)/shard_map/ppermute | solution.py:45
  73.6 3.1 %grad_img_rest.1 = (bf16[528,1280]{1,0:T(8,128)(2,1)S(1)}, bf16[512,1024]{1,0:T(8,128)(2,1)S(1)}) custom-call(f32[4]{0:T(128)S(1)} %pad_maximum_fusion.2.refs_2_.scale_ref, f32[1024,1024]{1,0:T(8,128)S(1)} %get-tuple-element.41.refs_3_.logit_ref, bf16[1024,1280]{1,0:T(8,128)(2,1)S(1)} %get-tuple-element.42.refs_4_.txt_ref, ...), custom_call_target="tpu_custom_call" | custom-call | flops 1342177280 | bytes 1048576 | tf_op jit(solution)/shard_map/grad_img_rest/pallas_call | solution.py:364
  76.7 0.4 pair.1
  77.1 1.3 %collective-permute-start.27 = (bf16[80,1280]{1,0:T(8,128)(2,1)S(1)}, bf16[80,1280]{1,0:T(8,128)(2,1)S(1)}, u32[]{:S(2)}, u32[]{:S(2)}) collective-permute-start(bf16[80,1280]{1,0:T(8,128)(2,1)S(1)} %get-tuple-element.52), channel_id=1, source_target_pairs={{0,7},{1,0},{2,1},{3,2},{4,3},{5,4},{6,5},{7,6},{8,15},{9,8},{10,9... | collective-permute-start | bytes 614408 | tf_op jit(solution)/shard_map/ppermute | solution.py:45
  78.4 0.9 grad_txt_far.1
  79.3 1.9 %collective-permute-start.30 = (bf16[128,1280]{1,0:T(8,128)(2,1)S(1)}, bf16[128,1280]{1,0:T(8,128)(2,1)S(1)}, u32[]{:S(2)}, u32[]{:S(2)}) collective-permute-start(bf16[128,1280]{1,0:T(8,128)(2,1)S(1)} %get-tuple-element.63), channel_id=1, source_target_pairs={{0,64},{1,65},{2,66},{3,67},{4,68},{5,69},{6,70},{7,71},{8,72},{9,... | collective-permute-start | bytes 983048 | tf_op jit(solution)/shard_map/ppermute | solution.py:45
  81.2 0.8 collective-permute-start.29
  82.1 2.9 %grad_txt.1 = (bf16[256,1280]{1,0:T(8,128)(2,1)S(1)}, bf16[256,1280]{1,0:T(8,128)(2,1)S(1)}, bf16[256,1280]{1,0:T(8,128)(2,1)S(1)}) custom-call(bf16[512,1024]{1,0:T(8,128)(2,1)S(1)} %get-tuple-element.53.low_ref, bf16[512,1024]{1,0:T(8,128)(2,1)S(1)} %get-tuple-element.54.high_ref, bf16[1024,1280]{1,0:T(8,128)(2,1)S(1)} %get-tuple-element.55.img_ref), custom_call_target="tpu_custom_call" | custom-call | flops 2013265920 | bytes 1048576 | tf_op jit(solution)/shard_map/grad_txt/pallas_call | solution.py:387
  85.0 0.1 collective-permute-start.28
  85.1 1.7 %collective-permute-done.30.high_ref = bf16[128,1280]{1,0:T(8,128)(2,1)S(1)} collective-permute-done((bf16[128,1280]{1,0:T(8,128)(2,1)S(1)}, bf16[128,1280]{1,0:T(8,128)(2,1)S(1)}, u32[]{:S(2)}, u32[]{:S(2)}) %collective-permute-start.30) | collective-permute-done | bytes 327712 | tf_op jit(solution)/shard_map/ppermute | solution.py:45
  86.8 1.1 collective-permute-done.29.low_ref
  87.9 0.2 plane_fold.1
  88.1 2.1 %collective-permute-start.35 = (bf16[272,1280]{1,0:T(8,128)(2,1)S(1)}, bf16[272,1280]{1,0:T(8,128)(2,1)S(1)}, u32[]{:S(2)}, u32[]{:S(2)}) collective-permute-start(bf16[272,1280]{1,0:T(8,128)(2,1)S(1)} %get-tuple-element.68), channel_id=1, source_target_pairs={{0,192},{1,193},{2,194},{3,195},{4,196},{5,197},{6,198},{7,199},{8... | collective-permute-start | bytes 2088968 | tf_op jit(solution)/shard_map/ppermute | solution.py:45
  90.2 2.4 %collective-permute-done.28.refs_1_ = bf16[144,1280]{1,0:T(8,128)(2,1)S(1)} collective-permute-done((bf16[144,1280]{1,0:T(8,128)(2,1)S(1)}, bf16[144,1280]{1,0:T(8,128)(2,1)S(1)}, u32[]{:S(2)}, u32[]{:S(2)}) %collective-permute-start.28) | collective-permute-done | bytes 368672 | tf_op jit(solution)/shard_map/ppermute | solution.py:45
  92.7 0.1 ring_fold.3
  92.8 7.9 %collective-permute-done.31.arrived_ref = bf16[144,1280]{1,0:T(8,128)(2,1)S(1)} collective-permute-done((bf16[144,1280]{1,0:T(8,128)(2,1)S(1)}, bf16[144,1280]{1,0:T(8,128)(2,1)S(1)}, u32[]{:S(2)}, u32[]{:S(2)}) %collective-permute-start.31) | collective-permute-done | bytes 368672 | tf_op jit(solution)/shard_map/ppermute | solution.py:45
  100.7 0.1 last_fold.1
  100.8 0.1 collective-permute-start.33
  100.9 0.7 collective-permute-done.36.up_ref
  101.6 0.2 line.1
  101.8 0.4 collective-permute-start.37
  102.3 1.1 collective-permute-start.38
  103.4 1.1 collective-permute-start.39
  104.5 2.2 %collective-permute-done.33.refs_3_ = bf16[80,1280]{1,0:T(8,128)(2,1)S(1)} collective-permute-done((bf16[80,1280]{1,0:T(8,128)(2,1)S(1)}, bf16[80,1280]{1,0:T(8,128)(2,1)S(1)}, u32[]{:S(2)}, u32[]{:S(2)}) %collective-permute-start.33) | collective-permute-done | bytes 204832 | tf_op jit(solution)/shard_map/ppermute | solution.py:45
  106.7 3.8 %collective-permute-start.34 = (bf16[80,1280]{1,0:T(8,128)(2,1)S(1)}, bf16[80,1280]{1,0:T(8,128)(2,1)S(1)}, u32[]{:S(2)}, u32[]{:S(2)}) collective-permute-start(bf16[80,1280]{1,0:T(8,128)(2,1)S(1)} %collective-permute-done.33.refs_3_), channel_id=1, source_target_pairs={{0,16},{1,17},{2,18},{3,19},{4,20},{5,21},{6,22},{7,23},{8,24},{9,... | collective-permute-start | bytes 614408 | tf_op jit(solution)/shard_map/ppermute | solution.py:45
  110.5 5.7 %collective-permute-done.32.refs_1_ = bf16[64,1280]{1,0:T(8,128)(2,1)S(1)} collective-permute-done((bf16[64,1280]{1,0:T(8,128)(2,1)S(1)}, bf16[64,1280]{1,0:T(8,128)(2,1)S(1)}, u32[]{:S(2)}, u32[]{:S(2)}) %collective-permute-start.32) | collective-permute-done | bytes 163872 | tf_op jit(solution)/shard_map/ppermute | solution.py:45
  116.2 1.7 %finish.1 = (bf16[64,1280]{1,0:T(8,128)(2,1)}, bf16[64,1280]{1,0:T(8,128)(2,1)}, f32[1]{0:T(128)}, f32[1]{0:T(128)}) custom-call(f32[4]{0:T(128)S(1)} %pad_maximum_fusion.2.refs_2_.scale_ref, bf16[64,1280]{1,0:T(8,128)(2,1)S(1)} %copy-done.1, bf16[64,1280]{1,0:T(8,128)(2,1)S(1)} %copy-done.3, bf16[64,1280]{1,0:T(8,128)(2,1)S(1)} %normalize_img.1.img_hat_ref.refs_12_, ...), custom_call_target="tpu_custom_call" | custom-call | bytes 1048576 | tf_op jit(solution)/shard_map/finish/pallas_call | solution.py:424
  (57 shorter events, 0.6 us)
Async XLA Ops:
  0.6 0.9 copy-start
  1.7 7.1 %collective-permute-start = (bf16[64,1280]{1,0:T(8,128)(2,1)S(1)}, bf16[64,1280]{1,0:T(8,128)(2,1)S(1)}, u32[]{:S(2)}, u32[]{:S(2)}) collective-permute-start(bf16[64,1280]{1,0:T(8,128)(2,1)S(1)} %normalize_img.1.img_hat_ref.refs_12_), channel_id=1, source_target_pairs={{0,16},{1,17},{2,18},{3,19},{4,20},{5,21},{6,22},{7,23},{8,24},{9,... | collective-permute-start | bytes 491528 | tf_op jit(solution)/shard_map/ppermute | solution.py:45
  5.0 0.9 copy-start.2
  5.9 24.2 %copy-start.4 = (s32[4]{0:T(128)S(1)}, s32[4]{0:T(128)}, u32[]{:S(2)}) copy-start(s32[4]{0:T(128)} %constant.90.clone) | copy-start | bytes 52
  6.1 8.4 %collective-permute-start.4 = (bf16[64,1280]{1,0:T(8,128)(2,1)S(1)}, bf16[64,1280]{1,0:T(8,128)(2,1)S(1)}, u32[]{:S(2)}, u32[]{:S(2)}) collective-permute-start(bf16[64,1280]{1,0:T(8,128)(2,1)S(1)} %normalize_txt.1.txt_hat_ref), channel_id=1, source_target_pairs={{0,32},{1,33},{2,34},{3,35},{4,36},{5,37},{6,38},{7,39},{8,40},{9,... | collective-permute-start | bytes 491528 | tf_op jit(solution)/shard_map/ppermute | solution.py:45
  7.3 7.2 %collective-permute-start.3 = (bf16[64,1280]{1,0:T(8,128)(2,1)S(1)}, bf16[64,1280]{1,0:T(8,128)(2,1)S(1)}, u32[]{:S(2)}, u32[]{:S(2)}) collective-permute-start(bf16[64,1280]{1,0:T(8,128)(2,1)S(1)} %normalize_txt.1.txt_hat_ref), channel_id=1, source_target_pairs={{0,40},{1,41},{2,42},{3,43},{4,44},{5,45},{6,46},{7,47},{8,0},{9,1... | collective-permute-start | bytes 491528 | tf_op jit(solution)/shard_map/ppermute | solution.py:45
  8.1 6.4 %collective-permute-start.2 = (bf16[64,1280]{1,0:T(8,128)(2,1)S(1)}, bf16[64,1280]{1,0:T(8,128)(2,1)S(1)}, u32[]{:S(2)}, u32[]{:S(2)}) collective-permute-start(bf16[64,1280]{1,0:T(8,128)(2,1)S(1)} %normalize_txt.1.txt_hat_ref), channel_id=1, source_target_pairs={{0,8},{1,9},{2,10},{3,11},{4,12},{5,13},{6,14},{7,15},{8,32},{9,33... | collective-permute-start | bytes 491528 | tf_op jit(solution)/shard_map/ppermute | solution.py:45
  8.8 28.7 %copy-start.5 = (s32[16]{0:T(128)S(1)}, s32[16]{0:T(128)}, u32[]{:S(2)}) copy-start(s32[16]{0:T(128)} %constant.92.clone) | copy-start | bytes 196
  8.8 28.7 %copy-start.6 = (s32[16]{0:T(128)S(1)}, s32[16]{0:T(128)}, u32[]{:S(2)}) copy-start(s32[16]{0:T(128)} %constant.91.clone) | copy-start | bytes 196
  8.9 9.7 %collective-permute-start.1 = (bf16[128,1280]{1,0:T(8,128)(2,1)S(1)}, bf16[128,1280]{1,0:T(8,128)(2,1)S(1)}, u32[]{:S(2)}, u32[]{:S(2)}) collective-permute-start(bf16[128,1280]{1,0:T(8,128)(2,1)S(1)} %pad_maximum_fusion.1), channel_id=1, source_target_pairs={{0,1},{1,2},{2,3},{3,4},{4,5},{5,6},{6,7},{7,0},{8,9},{9,10},{10,1... | collective-permute-start | bytes 983048 | tf_op jit(solution)/shard_map/ppermute | solution.py:45
  14.6 15.8 %collective-permute-start.10 = (bf16[256,1280]{1,0:T(8,128)(2,1)S(1)}, bf16[256,1280]{1,0:T(8,128)(2,1)S(1)}, u32[]{:S(2)}, u32[]{:S(2)}) collective-permute-start(bf16[256,1280]{1,0:T(8,128)(2,1)S(1)} %pad_maximum_fusion.refs_13_), channel_id=1, source_target_pairs={{0,192},{1,193},{2,194},{3,195},{4,196},{5,197},{6,198},{7,199},{8... | collective-permute-start | bytes 1966088 | tf_op jit(solution)/shard_map/ppermute | solution.py:45
  17.1 16.0 %collective-permute-start.9 = (bf16[256,1280]{1,0:T(8,128)(2,1)S(1)}, bf16[256,1280]{1,0:T(8,128)(2,1)S(1)}, u32[]{:S(2)}, u32[]{:S(2)}) collective-permute-start(bf16[256,1280]{1,0:T(8,128)(2,1)S(1)} %pad_maximum_fusion.refs_13_), channel_id=1, source_target_pairs={{0,64},{1,65},{2,66},{3,67},{4,68},{5,69},{6,70},{7,71},{8,72},{9,... | collective-permute-start | bytes 1966088 | tf_op jit(solution)/shard_map/ppermute | solution.py:45
  18.5 7.2 %collective-permute-start.6 = (bf16[128,1280]{1,0:T(8,128)(2,1)S(1)}, bf16[128,1280]{1,0:T(8,128)(2,1)S(1)}, u32[]{:S(2)}, u32[]{:S(2)}) collective-permute-start(bf16[128,1280]{1,0:T(8,128)(2,1)S(1)} %collective-permute-done.1.refs_8_), channel_id=1, source_target_pairs={{0,1},{1,2},{2,3},{3,4},{4,5},{5,6},{6,7},{7,0},{8,9},{9,10},{10,1... | collective-permute-start | bytes 983048 | tf_op jit(solution)/shard_map/ppermute | solution.py:45
  25.7 8.2 %collective-permute-start.8 = (bf16[128,1280]{1,0:T(8,128)(2,1)S(1)}, bf16[128,1280]{1,0:T(8,128)(2,1)S(1)}, u32[]{:S(2)}, u32[]{:S(2)}) collective-permute-start(bf16[128,1280]{1,0:T(8,128)(2,1)S(1)} %collective-permute-done.6.refs_9_), channel_id=1, source_target_pairs={{0,1},{1,2},{2,3},{3,4},{4,5},{5,6},{6,7},{7,0},{8,9},{9,10},{10,1... | collective-permute-start | bytes 983048 | tf_op jit(solution)/shard_map/ppermute | solution.py:45
  29.1 7.8 %collective-permute-start.5 = (bf16[128,1280]{1,0:T(8,128)(2,1)S(1)}, bf16[128,1280]{1,0:T(8,128)(2,1)}, u32[]{:S(2)}, u32[]{:S(2)}) collective-permute-start(bf16[128,1280]{1,0:T(8,128)(2,1)S(1)} %collective-permute-done.1.refs_8_), channel_id=1, source_target_pairs={{0,16},{1,17},{2,18},{3,19},{4,20},{5,21},{6,22},{7,23},{8,24},{9,... | collective-permute-start | bytes 983048 | tf_op jit(solution)/shard_map/ppermute | solution.py:45
  30.4 7.2 %collective-permute-start.14 = (bf16[128,1280]{1,0:T(8,128)(2,1)S(1)}, bf16[128,1280]{1,0:T(8,128)(2,1)S(1)}, u32[]{:S(2)}, u32[]{:S(2)}) collective-permute-start(bf16[128,1280]{1,0:T(8,128)(2,1)S(1)} %slice.9), channel_id=1, source_target_pairs={{0,192},{1,193},{2,194},{3,195},{4,196},{5,197},{6,198},{7,199},{8... | collective-permute-start | bytes 983048 | tf_op jit(solution)/shard_map/ppermute | solution.py:45
  33.1 7.5 %collective-permute-start.13 = (bf16[128,1280]{1,0:T(8,128)(2,1)S(1)}, bf16[128,1280]{1,0:T(8,128)(2,1)S(1)}, u32[]{:S(2)}, u32[]{:S(2)}) collective-permute-start(bf16[128,1280]{1,0:T(8,128)(2,1)S(1)} %slice.8), channel_id=1, source_target_pairs={{0,64},{1,65},{2,66},{3,67},{4,68},{5,69},{6,70},{7,71},{8,72},{9,... | collective-permute-start | bytes 983048 | tf_op jit(solution)/shard_map/ppermute | solution.py:45
  33.2 4.4 %collective-permute-start.7 = (bf16[128,1280]{1,0:T(8,128)(2,1)S(1)}, bf16[128,1280]{1,0:T(8,128)(2,1)S(1)}, u32[]{:S(2)}, u32[]{:S(2)}) collective-permute-start(bf16[128,1280]{1,0:T(8,128)(2,1)S(1)} %collective-permute-done.6.refs_9_), channel_id=1, source_target_pairs={{0,16},{1,17},{2,18},{3,19},{4,20},{5,21},{6,22},{7,23},{8,24},{9,... | collective-permute-start | bytes 983048 | tf_op jit(solution)/shard_map/ppermute | solution.py:45
  33.9 7.0 %collective-permute-start.12 = (bf16[128,1280]{1,0:T(8,128)(2,1)S(1)}, bf16[128,1280]{1,0:T(8,128)(2,1)S(1)}, u32[]{:S(2)}, u32[]{:S(2)}) collective-permute-start(bf16[128,1280]{1,0:T(8,128)(2,1)S(1)} %collective-permute-done.8.refs_10_), channel_id=1, source_target_pairs={{0,1},{1,2},{2,3},{3,4},{4,5},{5,6},{6,7},{7,0},{8,9},{9,10},{10,1... | collective-permute-start | bytes 983048 | tf_op jit(solution)/shard_map/ppermute | solution.py:45
  36.9 4.0 %collective-permute-start.11 = (bf16[128,1280]{1,0:T(8,128)(2,1)S(1)}, bf16[128,1280]{1,0:T(8,128)(2,1)S(1)}, u32[]{:S(2)}, u32[]{:S(2)}) collective-permute-start(bf16[128,1280]{1,0:T(8,128)(2,1)S(1)} %collective-permute-done.8.refs_10_), channel_id=1, source_target_pairs={{0,16},{1,17},{2,18},{3,19},{4,20},{5,21},{6,22},{7,23},{8,24},{9,... | collective-permute-start | bytes 983048 | tf_op jit(solution)/shard_map/ppermute | solution.py:45
  46.1 5.7 %collective-permute-start.15 = (f32[24,128]{1,0:T(8,128)S(1)}, f32[24,128]{1,0:T(8,128)S(1)}, u32[]{:S(2)}, u32[]{:S(2)}) collective-permute-start(f32[24,128]{1,0:T(8,128)S(1)} %get-tuple-element.43), channel_id=1, source_target_pairs={{0,16},{1,17},{2,18},{3,19},{4,20},{5,21},{6,22},{7,23},{8,24},{9,... | collective-permute-start | bytes 36872 | tf_op jit(solution)/shard_map/ppermute | solution.py:45
  51.9 3.8 %collective-permute-start.17 = (f32[24,128]{1,0:T(8,128)S(1)}, f32[24,128]{1,0:T(8,128)S(1)}, u32[]{:S(2)}, u32[]{:S(2)}) collective-permute-start(f32[24,128]{1,0:T(8,128)S(1)} %add.94), channel_id=1, source_target_pairs={{0,7},{1,0},{2,1},{3,2},{4,3},{5,4},{6,5},{7,6},{8,15},{9,8},{10,9... | collective-permute-start | bytes 36872 | tf_op jit(solution)/shard_map/ppermute | solution.py:45
  51.9 3.8 %collective-permute-start.16 = (f32[24,128]{1,0:T(8,128)S(1)}, f32[24,128]{1,0:T(8,128)S(1)}, u32[]{:S(2)}, u32[]{:S(2)}) collective-permute-start(f32[24,128]{1,0:T(8,128)S(1)} %add.94), channel_id=1, source_target_pairs={{0,1},{1,2},{2,3},{3,4},{4,5},{5,6},{6,7},{7,0},{8,9},{9,10},{10,1... | collective-permute-start | bytes 36872 | tf_op jit(solution)/shard_map/ppermute | solution.py:45
  53.3 5.7 %collective-permute-start.22 = (f32[16,128]{1,0:T(8,128)S(1)}, f32[16,128]{1,0:T(8,128)S(1)}, u32[]{:S(2)}, u32[]{:S(2)}) collective-permute-start(f32[16,128]{1,0:T(8,128)S(1)} %get-tuple-element.44), channel_id=1, source_target_pairs={{0,40},{1,41},{2,42},{3,43},{4,44},{5,45},{6,46},{7,47},{8,0},{9,1... | collective-permute-start | bytes 24584 | tf_op jit(solution)/shard_map/ppermute | solution.py:45
  55.0 4.0 %collective-permute-start.21 = (f32[16,128]{1,0:T(8,128)S(1)}, f32[16,128]{1,0:T(8,128)S(1)}, u32[]{:S(2)}, u32[]{:S(2)}) collective-permute-start(f32[16,128]{1,0:T(8,128)S(1)} %get-tuple-element.44), channel_id=1, source_target_pairs={{0,32},{1,33},{2,34},{3,35},{4,36},{5,37},{6,38},{7,39},{8,40},{9,... | collective-permute-start | bytes 24584 | tf_op jit(solution)/shard_map/ppermute | solution.py:45
  55.1 4.0 %collective-permute-start.20 = (f32[16,128]{1,0:T(8,128)S(1)}, f32[16,128]{1,0:T(8,128)S(1)}, u32[]{:S(2)}, u32[]{:S(2)}) collective-permute-start(f32[16,128]{1,0:T(8,128)S(1)} %get-tuple-element.44), channel_id=1, source_target_pairs={{0,8},{1,9},{2,10},{3,11},{4,12},{5,13},{6,14},{7,15},{8,32},{9,33... | collective-permute-start | bytes 24584 | tf_op jit(solution)/shard_map/ppermute | solution.py:45
  55.6 10.4 %collective-permute-start.19 = (f32[24,128]{1,0:T(8,128)S(1)}, f32[24,128]{1,0:T(8,128)S(1)}, u32[]{:S(2)}, u32[]{:S(2)}) collective-permute-start(f32[24,128]{1,0:T(8,128)S(1)} %get-tuple-element.75), channel_id=1, source_target_pairs={{0,5},{1,6},{2,7},{3,0},{4,1},{5,2},{6,3},{7,4},{8,13},{9,14},{10,... | collective-permute-start | bytes 36872 | tf_op jit(solution)/shard_map/ppermute | solution.py:45
  59.0 7.1 %collective-permute-start.18 = (f32[24,128]{1,0:T(8,128)S(1)}, f32[24,128]{1,0:T(8,128)S(1)}, u32[]{:S(2)}, u32[]{:S(2)}) collective-permute-start(f32[24,128]{1,0:T(8,128)S(1)} %get-tuple-element.74.refs_5_), channel_id=1, source_target_pairs={{0,3},{1,4},{2,5},{3,6},{4,7},{5,0},{6,1},{7,2},{8,11},{9,12},{10,... | collective-permute-start | bytes 36872 | tf_op jit(solution)/shard_map/ppermute | solution.py:45
  59.0 3.9 %collective-permute-start.25 = (f32[16,128]{1,0:T(8,128)S(1)}, f32[16,128]{1,0:T(8,128)S(1)}, u32[]{:S(2)}, u32[]{:S(2)}) collective-permute-start(f32[16,128]{1,0:T(8,128)S(1)} %add_add_fusion.refs_8_), channel_id=1, source_target_pairs={{0,192},{1,193},{2,194},{3,195},{4,196},{5,197},{6,198},{7,199},{8... | collective-permute-start | bytes 24584 | tf_op jit(solution)/shard_map/ppermute | solution.py:45
  62.1 4.0 %collective-permute-start.24 = (f32[16,128]{1,0:T(8,128)S(1)}, f32[16,128]{1,0:T(8,128)S(1)}, u32[]{:S(2)}, u32[]{:S(2)}) collective-permute-start(f32[16,128]{1,0:T(8,128)S(1)} %add_add_fusion.refs_8_), channel_id=1, source_target_pairs={{0,128},{1,129},{2,130},{3,131},{4,132},{5,133},{6,134},{7,135},{8... | collective-permute-start | bytes 24584 | tf_op jit(solution)/shard_map/ppermute | solution.py:45
  62.2 3.9 %collective-permute-start.23 = (f32[16,128]{1,0:T(8,128)S(1)}, f32[16,128]{1,0:T(8,128)S(1)}, u32[]{:S(2)}, u32[]{:S(2)}) collective-permute-start(f32[16,128]{1,0:T(8,128)S(1)} %add_add_fusion.refs_8_), channel_id=1, source_target_pairs={{0,64},{1,65},{2,66},{3,67},{4,68},{5,69},{6,70},{7,71},{8,72},{9,... | collective-permute-start | bytes 24584 | tf_op jit(solution)/shard_map/ppermute | solution.py:45
  69.4 7.4 %collective-permute-start.26 = (bf16[528,1280]{1,0:T(8,128)(2,1)S(1)}, bf16[528,1280]{1,0:T(8,128)(2,1)S(1)}, u32[]{:S(2)}, u32[]{:S(2)}) collective-permute-start(bf16[528,1280]{1,0:T(8,128)(2,1)S(1)} %get-tuple-element.49), channel_id=1, source_target_pairs={{0,16},{1,17},{2,18},{3,19},{4,20},{5,21},{6,22},{7,23},{8,24},{9,... | collective-permute-start | bytes 4055048 | tf_op jit(solution)/shard_map/ppermute | solution.py:45
  77.1 7.8 %collective-permute-start.27 = (bf16[80,1280]{1,0:T(8,128)(2,1)S(1)}, bf16[80,1280]{1,0:T(8,128)(2,1)S(1)}, u32[]{:S(2)}, u32[]{:S(2)}) collective-permute-start(bf16[80,1280]{1,0:T(8,128)(2,1)S(1)} %get-tuple-element.52), channel_id=1, source_target_pairs={{0,7},{1,0},{2,1},{3,2},{4,3},{5,4},{6,5},{7,6},{8,15},{9,8},{10,9... | collective-permute-start | bytes 614408 | tf_op jit(solution)/shard_map/ppermute | solution.py:45
  79.3 7.5 %collective-permute-start.30 = (bf16[128,1280]{1,0:T(8,128)(2,1)S(1)}, bf16[128,1280]{1,0:T(8,128)(2,1)S(1)}, u32[]{:S(2)}, u32[]{:S(2)}) collective-permute-start(bf16[128,1280]{1,0:T(8,128)(2,1)S(1)} %get-tuple-element.63), channel_id=1, source_target_pairs={{0,64},{1,65},{2,66},{3,67},{4,68},{5,69},{6,70},{7,71},{8,72},{9,... | collective-permute-start | bytes 983048 | tf_op jit(solution)/shard_map/ppermute | solution.py:45
  81.2 6.7 %collective-permute-start.29 = (bf16[144,1280]{1,0:T(8,128)(2,1)S(1)}, bf16[144,1280]{1,0:T(8,128)(2,1)S(1)}, u32[]{:S(2)}, u32[]{:S(2)}) collective-permute-start(bf16[144,1280]{1,0:T(8,128)(2,1)S(1)} %get-tuple-element.62), channel_id=1, source_target_pairs={{0,192},{1,193},{2,194},{3,195},{4,196},{5,197},{6,198},{7,199},{8... | collective-permute-start | bytes 1105928 | tf_op jit(solution)/shard_map/ppermute | solution.py:45
  85.0 7.6 %collective-permute-start.28 = (bf16[144,1280]{1,0:T(8,128)(2,1)S(1)}, bf16[144,1280]{1,0:T(8,128)(2,1)S(1)}, u32[]{:S(2)}, u32[]{:S(2)}) collective-permute-start(bf16[144,1280]{1,0:T(8,128)(2,1)S(1)} %ring_fold.2), channel_id=1, source_target_pairs={{0,7},{1,0},{2,1},{3,2},{4,3},{5,4},{6,5},{7,6},{8,15},{9,8},{10,9... | collective-permute-start | bytes 1105928 | tf_op jit(solution)/shard_map/ppermute | solution.py:45
  88.1 12.8 %collective-permute-start.35 = (bf16[272,1280]{1,0:T(8,128)(2,1)S(1)}, bf16[272,1280]{1,0:T(8,128)(2,1)S(1)}, u32[]{:S(2)}, u32[]{:S(2)}) collective-permute-start(bf16[272,1280]{1,0:T(8,128)(2,1)S(1)} %get-tuple-element.68), channel_id=1, source_target_pairs={{0,192},{1,193},{2,194},{3,195},{4,196},{5,197},{6,198},{7,199},{8... | collective-permute-start | bytes 2088968 | tf_op jit(solution)/shard_map/ppermute | solution.py:45
  90.2 11.4 %collective-permute-start.36 = (bf16[272,1280]{1,0:T(8,128)(2,1)S(1)}, bf16[272,1280]{1,0:T(8,128)(2,1)S(1)}, u32[]{:S(2)}, u32[]{:S(2)}) collective-permute-start(bf16[272,1280]{1,0:T(8,128)(2,1)S(1)} %get-tuple-element.64), channel_id=1, source_target_pairs={{0,64},{1,65},{2,66},{3,67},{4,68},{5,69},{6,70},{7,71},{8,72},{9,... | collective-permute-start | bytes 2088968 | tf_op jit(solution)/shard_map/ppermute | solution.py:45
  92.8 7.9 %collective-permute-start.31 = (bf16[144,1280]{1,0:T(8,128)(2,1)S(1)}, bf16[144,1280]{1,0:T(8,128)(2,1)S(1)}, u32[]{:S(2)}, u32[]{:S(2)}) collective-permute-start(bf16[144,1280]{1,0:T(8,128)(2,1)S(1)} %ring_fold.3), channel_id=1, source_target_pairs={{0,7},{1,0},{2,1},{3,2},{4,3},{5,4},{6,5},{7,6},{8,15},{9,8},{10,9... | collective-permute-start | bytes 1105928 | tf_op jit(solution)/shard_map/ppermute | solution.py:45
  100.8 15.4 %copy-start.1 = (bf16[64,1280]{1,0:T(8,128)(2,1)S(1)}, bf16[64,1280]{1,0:T(8,128)(2,1)}, u32[]{:S(2)}) copy-start(bf16[64,1280]{1,0:T(8,128)(2,1)} %img_ref.1) | copy-start | bytes 491524
  100.8 15.4 %copy-start.3 = (bf16[64,1280]{1,0:T(8,128)(2,1)S(1)}, bf16[64,1280]{1,0:T(8,128)(2,1)}, u32[]{:S(2)}) copy-start(bf16[64,1280]{1,0:T(8,128)(2,1)} %txt_ref.1) | copy-start | bytes 491524
  100.8 5.9 %collective-permute-start.33 = (bf16[80,1280]{1,0:T(8,128)(2,1)S(1)}, bf16[80,1280]{1,0:T(8,128)(2,1)S(1)}, u32[]{:S(2)}, u32[]{:S(2)}) collective-permute-start(bf16[80,1280]{1,0:T(8,128)(2,1)S(1)} %get-tuple-element.67), channel_id=1, source_target_pairs={{0,7},{1,0},{2,1},{3,2},{4,3},{5,4},{6,5},{7,6},{8,15},{9,8},{10,9... | collective-permute-start | bytes 614408 | tf_op jit(solution)/shard_map/ppermute | solution.py:45
  101.8 8.6 %collective-permute-start.37 = (bf16[80,1280]{1,0:T(8,128)(2,1)S(1)}, bf16[80,1280]{1,0:T(8,128)(2,1)S(1)}, u32[]{:S(2)}, u32[]{:S(2)}) collective-permute-start(bf16[80,1280]{1,0:T(8,128)(2,1)S(1)} %get-tuple-element.70), channel_id=1, source_target_pairs={{0,40},{1,41},{2,42},{3,43},{4,44},{5,45},{6,46},{7,47},{8,0},{9,1... | collective-permute-start | bytes 614408 | tf_op jit(solution)/shard_map/ppermute | solution.py:45
  102.3 8.2 %collective-permute-start.38 = (bf16[80,1280]{1,0:T(8,128)(2,1)S(1)}, bf16[80,1280]{1,0:T(8,128)(2,1)S(1)}, u32[]{:S(2)}, u32[]{:S(2)}) collective-permute-start(bf16[80,1280]{1,0:T(8,128)(2,1)S(1)} %get-tuple-element.71), channel_id=1, source_target_pairs={{0,8},{1,9},{2,10},{3,11},{4,12},{5,13},{6,14},{7,15},{8,32},{9,33... | collective-permute-start | bytes 614408 | tf_op jit(solution)/shard_map/ppermute | solution.py:45
  103.4 7.1 %collective-permute-start.39 = (bf16[80,1280]{1,0:T(8,128)(2,1)S(1)}, bf16[80,1280]{1,0:T(8,128)(2,1)S(1)}, u32[]{:S(2)}, u32[]{:S(2)}) collective-permute-start(bf16[80,1280]{1,0:T(8,128)(2,1)S(1)} %get-tuple-element.72), channel_id=1, source_target_pairs={{0,32},{1,33},{2,34},{3,35},{4,36},{5,37},{6,38},{7,39},{8,40},{9,... | collective-permute-start | bytes 614408 | tf_op jit(solution)/shard_map/ppermute | solution.py:45
  106.7 9.5 %collective-permute-start.34 = (bf16[80,1280]{1,0:T(8,128)(2,1)S(1)}, bf16[80,1280]{1,0:T(8,128)(2,1)S(1)}, u32[]{:S(2)}, u32[]{:S(2)}) collective-permute-start(bf16[80,1280]{1,0:T(8,128)(2,1)S(1)} %collective-permute-done.33.refs_3_), channel_id=1, source_target_pairs={{0,16},{1,17},{2,18},{3,19},{4,20},{5,21},{6,22},{7,23},{8,24},{9,... | collective-permute-start | bytes 614408 | tf_op jit(solution)/shard_map/ppermute | solution.py:45
  110.5 5.7 %collective-permute-start.32 = (bf16[64,1280]{1,0:T(8,128)(2,1)S(1)}, bf16[64,1280]{1,0:T(8,128)(2,1)S(1)}, u32[]{:S(2)}, u32[]{:S(2)}) collective-permute-start(bf16[64,1280]{1,0:T(8,128)(2,1)S(1)} %get-tuple-element.66), channel_id=1, source_target_pairs={{0,7},{1,0},{2,1},{3,2},{4,3},{5,4},{6,5},{7,6},{8,15},{9,8},{10,9... | collective-permute-start | bytes 491528 | tf_op jit(solution)/shard_map/ppermute | solution.py:45
where the time goes:
time: 118 us
  starting transfers between devices  60.9 us (52%)
  waiting for transfers between devices  34.4 us (29%)
  Pallas kernels  18.6 us (16%)
  local copies, waits for them, and re-layouts  2.07 us (2%)
  between operations  1.77 us (2%)
    ppermute x40, starting transfers between devices, permute(): return lax.ppermute(array, AXES, pairs)  60.9 us
    ppermute x40, waiting for transfers between devices, permute(): return lax.ppermute(array, AXES, pairs)  34.4 us
    pallas_call x1, Pallas kernels, per_device(): call(lambda *refs: logits_kernel(img_order, txt_order, *refs), (shape(tot...  5.2 us
    pallas_call x1, Pallas kernels, per_device(): call(grad_img_kernel, half_grad + (shape(total, 128, dtype=F32), shape(8,...  3.29 us
    pallas_call x1, Pallas kernels, per_device(): call(grad_img_rest_kernel, half_grad, [SMEM] + [VMEM] * 5, 'grad_img_rest...  3.15 us
    pallas_call x1, Pallas kernels, per_device(): call(grad_txt_kernel, (shape(256, width),) * 3, [VMEM] * 3, 'grad_txt', f...  2.87 us
  transfers between devices with their start and end apart: 40, of which 13 were waited for; matrix products, arithmetic and copies ran while one was open for 0% of the time, Pallas kernels for 7%

commit v1 on v0

--- a/solution.py
+++ b/solution.py
@@ -154,22 +154,34 @@
         target[pl.ds(pl.multiple_of(at + k * 32, 32), 32), :] = source[cut, :]
 
 
-def logits_kernel(img_order, txt_order, *refs):
+def txt_tile(refs, step):
+    if step < 3:
+        return refs[step][...]
+    return jnp.concatenate([refs[3][...], refs[4][...]], axis=0)
+
+
+def gather_txt_kernel(*refs):
+    at = 0
+    for ref in refs[:-1]:
+        copy_rows(ref, 0, refs[-1], at, ref.shape[0])
+        at += ref.shape[0]
+
+
+def logits_kernel(img_order, *refs):
     row_place, col_place, scale_ref, diag_ref = refs[:4]
     n_img, n_txt = 9, 5
     img_refs, txt_refs = refs[4 : 4 + n_img], refs[4 + n_img : 4 + n_img + n_txt]
-    img_all, txt_all, logit_ref, row_ref, col_ref = refs[4 + n_img + n_txt :]
+    img_all, logit_ref, row_ref, col_ref = refs[4 + n_img + n_txt :]
     tile = 256
-    for blocks, order, target in ((img_refs, img_order, img_all), (txt_refs, txt_order, txt_all)):
-        at = 0
-        for k, first, size in order:
-            copy_rows(blocks[k], first, target, at, size)
-            at += size
+    at = 0
+    for k, first, size in img_order:
+        copy_rows(img_refs[k], first, img_all, at, size)
+        at += size
     row_sums, row_slopes = [], []
     for step in range(4):
         cut = slice(step * tile, (step + 1) * tile)
         logits = lax.dot_general(
-            img_all[...], txt_all[cut, :], (((1,), (1,)), ((), ())), preferred_element_type=F32
+            img_all[...], txt_tile(txt_refs, step), (((1,), (1,)), ((), ())), preferred_element_type=F32
         )
         logit_ref[:, cut] = logits
         powers = jnp.exp2(logits * scale_ref[2] - scale_ref[3])
@@ -191,6 +203,18 @@
 
 
 def grad_img_tiles(half, scale_ref, logit_ref, txt_ref, row_half, col_half, grad_ref, dlogit_ref):
+    @pl.loop(0, 2)
+    def _(step):
+        cut = pl.ds(pl.multiple_of(step * 256, 256), 256)
+        rows = pl.ds(pl.multiple_of(half * 512 + step * 256, 256), 256)
+        powers = jnp.exp2(logit_ref[rows, :] * scale_ref[2] - scale_ref[3])
+        by_row = jnp.concatenate([row_half[rows, :]] * 8, axis=1)
+        dlogit = (powers * (by_row + col_half[0:1, :])).astype(BF16)
+        dlogit_ref[cut, :] = dlogit
+        grad_ref[cut, :] = jnp.dot(dlogit, txt_ref[...], preferred_element_type=F32).astype(BF16)
+
+
+def grad_img_columns(half, scale_ref, logit_ref, txt_ref, row_half, col_half, grad_ref, dlogit_ref):
     rows = slice(half * 512, (half + 1) * 512)
     powers = jnp.exp2(logit_ref[rows, :] * scale_ref[2] - scale_ref[3])
     by_row = jnp.concatenate([row_half[rows, :]] * 8, axis=1)
@@ -229,7 +253,7 @@
 
 def grad_img_rest_kernel(scale_ref, logit_ref, txt_ref, row_half, col_half, scalar_ref, grad_ref, dlogit_ref):
     encode(grad_ref, 512, scalar_ref[...])
-    grad_img_tiles(1, scale_ref, logit_ref, txt_ref, row_half, col_half, grad_ref, dlogit_ref)
+    grad_img_columns(1, scale_ref, logit_ref, txt_ref, row_half, col_half, grad_ref, dlogit_ref)
 
 
 def grad_txt_tile(start, low_ref, high_ref, img_ref):
@@ -325,13 +349,11 @@
     img_order = [(0, 0, 128), (1, 0, 128), (2, 0, 128), (7, 64, 64), (3, 0, 64)]
     img_order += [(4, 0, 128), (5, 0, 128), (6, 0, 128), (7, 0, 64), (8, 0, 64)]
     txt_blocks = [line, up, down, low_far, high_far]
-    txt_order = [(k, 0, block.shape[0]) for k, block in enumerate(txt_blocks)]
 
     flops = 2 * total * total * width
-    img_all, txt_all, logits, row_part, col_part = call(
-        lambda *refs: logits_kernel(img_order, txt_order, *refs),
+    img_all, logits, row_part, col_part = call(
+        lambda *refs: logits_kernel(img_order, *refs),
         (
-            shape(total, width),
             shape(total, width),
             shape(total, total, dtype=F32),
             shape(24, 128, dtype=F32),
@@ -341,6 +363,7 @@
         "logits",
         flops,
     )(row_place, col_place, scales, diag, *img_blocks, *txt_blocks)
+    txt_all = call(gather_txt_kernel, shape(total, width), [VMEM] * len(txt_blocks), "gather_txt")(*txt_blocks)
 
     row_pair = row_part + to_sibling(row_part)
     col_line = col_part + along(col_part, "x", 1) + along(col_part, "x", 2) + along(col_part, "x", 3)

time: 118 us -> 117 us (level)
    pallas_call x1 -> x2, Pallas kernels: 5.2 us -> 5.14 us  [the longest x1 4.87 us: per_device(): call(lambda *refs: logits_kernel(img_order, *refs), (shape(total, width),...]
where the time goes in v1:
time: 117 us
  starting transfers between devices  60.9 us (52%)
  waiting for transfers between devices  34.2 us (29%)
  Pallas kernels  18 us (15%)
  local copies, waits for them, and re-layouts  2.07 us (2%)
  between operations  1.79 us (2%)
    ppermute x40, starting transfers between devices, permute(): return lax.ppermute(array, AXES, pairs)  60.9 us
    ppermute x40, waiting for transfers between devices, permute(): return lax.ppermute(array, AXES, pairs)  34.2 us
    pallas_call x1, Pallas kernels, per_device(): call(lambda *refs: logits_kernel(img_order, *refs), (shape(total, width),...  4.87 us
    pallas_call x1, Pallas kernels, per_device(): call(grad_img_rest_kernel, half_grad, [SMEM] + [VMEM] * 5, 'grad_img_rest...  3.14 us
    pallas_call x1, Pallas kernels, per_device(): call(grad_txt_kernel, (shape(256, width),) * 3, [VMEM] * 3, 'grad_txt', f...  2.85 us
    pallas_call x1, Pallas kernels, per_device(): call(grad_img_kernel, half_grad + (shape(total, 128, dtype=F32), shape(8,...  2.76 us
  transfers between devices with their start and end apart: 40, of which 13 were waited for; matrix products, arithmetic and copies ran while one was open for 0% of the time, Pallas kernels for 7%

profile of v1, /device:TPU:1, one launch (start us, length us, event | category | flops | bytes accessed | tf_op | source)
XLA Modules:
  0.0 117.2 jit_solution(11185398198468529731)
XLA Ops:
  0.6 0.9 copy-done
  1.5 0.1 normalize_img.1.img_hat_ref.refs_12_
  1.7 3.3 %collective-permute-start = (bf16[64,1280]{1,0:T(8,128)(2,1)S(1)}, bf16[64,1280]{1,0:T(8,128)(2,1)S(1)}, u32[]{:S(2)}, u32[]{:S(2)}) collective-permute-start(bf16[64,1280]{1,0:T(8,128)(2,1)S(1)} %normalize_img.1.img_hat_ref.refs_12_), channel_id=1, source_target_pairs={{0,16},{1,17},{2,18},{3,19},{4,20},{5,21},{6,22},{7,23},{8,24},{9,... | collective-permute-start | bytes 491528 | tf_op jit(solution)/shard_map/ppermute | solution.py:45
  5.0 0.9 copy-done.2
  5.9 0.1 normalize_txt.1.txt_hat_ref
  6.1 1.3 %collective-permute-start.4 = (bf16[64,1280]{1,0:T(8,128)(2,1)S(1)}, bf16[64,1280]{1,0:T(8,128)(2,1)S(1)}, u32[]{:S(2)}, u32[]{:S(2)}) collective-permute-start(bf16[64,1280]{1,0:T(8,128)(2,1)S(1)} %normalize_txt.1.txt_hat_ref), channel_id=1, source_target_pairs={{0,32},{1,33},{2,34},{3,35},{4,36},{5,37},{6,38},{7,39},{8,40},{9,... | collective-permute-start | bytes 491528 | tf_op jit(solution)/shard_map/ppermute | solution.py:45
  7.3 0.8 collective-permute-start.3
  8.1 0.7 collective-permute-start.2
  8.9 5.7 %collective-permute-start.1 = (bf16[128,1280]{1,0:T(8,128)(2,1)S(1)}, bf16[128,1280]{1,0:T(8,128)(2,1)S(1)}, u32[]{:S(2)}, u32[]{:S(2)}) collective-permute-start(bf16[128,1280]{1,0:T(8,128)(2,1)S(1)} %pad_maximum_fusion.1), channel_id=1, source_target_pairs={{0,1},{1,2},{2,3},{3,4},{4,5},{5,6},{6,7},{7,0},{8,9},{9,10},{10,1... | collective-permute-start | bytes 983048 | tf_op jit(solution)/shard_map/ppermute | solution.py:45
  14.6 2.6 %collective-permute-start.10 = (bf16[256,1280]{1,0:T(8,128)(2,1)S(1)}, bf16[256,1280]{1,0:T(8,128)(2,1)S(1)}, u32[]{:S(2)}, u32[]{:S(2)}) collective-permute-start(bf16[256,1280]{1,0:T(8,128)(2,1)S(1)} %pad_maximum_fusion.refs_13_.refs_0_), channel_id=1, source_target_pairs={{0,192},{1,193},{2,194},{3,195},{4,196},{5,197},{6,198},{7,199},{8... | collective-permute-start | bytes 1966088 | tf_op jit(solution)/shard_map/ppermute | solution.py:45
  17.1 1.4 %collective-permute-done.1.refs_8_ = bf16[128,1280]{1,0:T(8,128)(2,1)S(1)} collective-permute-done((bf16[128,1280]{1,0:T(8,128)(2,1)S(1)}, bf16[128,1280]{1,0:T(8,128)(2,1)S(1)}, u32[]{:S(2)}, u32[]{:S(2)}) %collective-permute-start.1) | collective-permute-done | bytes 327712 | tf_op jit(solution)/shard_map/ppermute | solution.py:45
  18.5 3.1 %collective-permute-start.6 = (bf16[128,1280]{1,0:T(8,128)(2,1)S(1)}, bf16[128,1280]{1,0:T(8,128)(2,1)S(1)}, u32[]{:S(2)}, u32[]{:S(2)}) collective-permute-start(bf16[128,1280]{1,0:T(8,128)(2,1)S(1)} %collective-permute-done.1.refs_8_), channel_id=1, source_target_pairs={{0,1},{1,2},{2,3},{3,4},{4,5},{5,6},{6,7},{7,0},{8,9},{9,10},{10,1... | collective-permute-start | bytes 983048 | tf_op jit(solution)/shard_map/ppermute | solution.py:45
  21.7 4.0 %collective-permute-done.6.refs_9_ = bf16[128,1280]{1,0:T(8,128)(2,1)S(1)} collective-permute-done((bf16[128,1280]{1,0:T(8,128)(2,1)S(1)}, bf16[128,1280]{1,0:T(8,128)(2,1)S(1)}, u32[]{:S(2)}, u32[]{:S(2)}) %collective-permute-start.6) | collective-permute-done | bytes 327712 | tf_op jit(solution)/shard_map/ppermute | solution.py:45
  25.7 3.4 %collective-permute-start.8 = (bf16[128,1280]{1,0:T(8,128)(2,1)S(1)}, bf16[128,1280]{1,0:T(8,128)(2,1)S(1)}, u32[]{:S(2)}, u32[]{:S(2)}) collective-permute-start(bf16[128,1280]{1,0:T(8,128)(2,1)S(1)} %collective-permute-done.6.refs_9_), channel_id=1, source_target_pairs={{0,1},{1,2},{2,3},{3,4},{4,5},{5,6},{6,7},{7,0},{8,9},{9,10},{10,1... | collective-permute-start | bytes 983048 | tf_op jit(solution)/shard_map/ppermute | solution.py:45
  29.2 0.2 diagonal.1.refs_3_
  30.2 0.1 add.91
  30.3 0.1 add.86
  30.4 2.7 %collective-permute-start.14 = (bf16[128,1280]{1,0:T(8,128)(2,1)S(1)}, bf16[128,1280]{1,0:T(8,128)(2,1)S(1)}, u32[]{:S(2)}, u32[]{:S(2)}) collective-permute-start(bf16[128,1280]{1,0:T(8,128)(2,1)S(1)} %slice.9), channel_id=1, source_target_pairs={{0,192},{1,193},{2,194},{3,195},{4,196},{5,197},{6,198},{7,199},{8... | collective-permute-start | bytes 983048 | tf_op jit(solution)/shard_map/ppermute | solution.py:45
  33.1 0.1 collective-permute-start.13
  33.2 0.7 collective-permute-start.7
  33.9 3.0 %collective-permute-start.12 = (bf16[128,1280]{1,0:T(8,128)(2,1)S(1)}, bf16[128,1280]{1,0:T(8,128)(2,1)S(1)}, u32[]{:S(2)}, u32[]{:S(2)}) collective-permute-start(bf16[128,1280]{1,0:T(8,128)(2,1)S(1)} %collective-permute-done.8.refs_10_), channel_id=1, source_target_pairs={{0,1},{1,2},{2,3},{3,4},{4,5},{5,6},{6,7},{7,0},{8,9},{9,10},{10,1... | collective-permute-start | bytes 983048 | tf_op jit(solution)/shard_map/ppermute | solution.py:45
  36.9 0.6 collective-permute-start.11
  37.6 3.0 %collective-permute-done.13.refs_16_.refs_3_ = bf16[128,1280]{1,0:T(8,128)(2,1)S(1)} collective-permute-done((bf16[128,1280]{1,0:T(8,128)(2,1)S(1)}, bf16[128,1280]{1,0:T(8,128)(2,1)S(1)}, u32[]{:S(2)}, u32[]{:S(2)}) %collective-permute-start.13) | collective-permute-done | bytes 327712 | tf_op jit(solution)/shard_map/ppermute | solution.py:45
  40.6 0.3 collective-permute-done.12.refs_11_
  40.9 4.9 %logits.1 = (bf16[1024,1280]{1,0:T(8,128)(2,1)S(1)}, f32[1024,1024]{1,0:T(8,128)S(1)}, f32[24,128]{1,0:T(8,128)S(1)}, f32[16,128]{1,0:T(8,128)S(1)}) custom-call(s32[16]{0:T(128)S(1)} %get-tuple-element.76.refs_0_, s32[16]{0:T(128)S(1)} %get-tuple-element.77.refs_1_, f32[4]{0:T(128)S(1)} %pad_maximum_fusion.2.refs_2_.scale_ref, ...), custom_call_target="tpu_custom_call" | custom-call | flops 2684354560 | bytes 1048576 | tf_op jit(solution)/shard_map/logits/pallas_call | solution.py:354
  45.8 4.9 %collective-permute-start.15 = (f32[24,128]{1,0:T(8,128)S(1)}, f32[24,128]{1,0:T(8,128)S(1)}, u32[]{:S(2)}, u32[]{:S(2)}) collective-permute-start(f32[24,128]{1,0:T(8,128)S(1)} %get-tuple-element.41), channel_id=1, source_target_pairs={{0,16},{1,17},{2,18},{3,19},{4,20},{5,21},{6,22},{7,23},{8,24},{9,... | collective-permute-start | bytes 36872 | tf_op jit(solution)/shard_map/ppermute | solution.py:45
  50.7 0.8 collective-permute-done.15
  51.5 1.5 %collective-permute-start.16 = (f32[24,128]{1,0:T(8,128)S(1)}, f32[24,128]{1,0:T(8,128)S(1)}, u32[]{:S(2)}, u32[]{:S(2)}) collective-permute-start(f32[24,128]{1,0:T(8,128)S(1)} %add.94), channel_id=1, source_target_pairs={{0,1},{1,2},{2,3},{3,4},{4,5},{5,6},{6,7},{7,0},{8,9},{9,10},{10,1... | collective-permute-start | bytes 36872 | tf_op jit(solution)/shard_map/ppermute | solution.py:45
  53.0 1.7 %collective-permute-start.22 = (f32[16,128]{1,0:T(8,128)S(1)}, f32[16,128]{1,0:T(8,128)S(1)}, u32[]{:S(2)}, u32[]{:S(2)}) collective-permute-start(f32[16,128]{1,0:T(8,128)S(1)} %get-tuple-element.42), channel_id=1, source_target_pairs={{0,40},{1,41},{2,42},{3,43},{4,44},{5,45},{6,46},{7,47},{8,0},{9,1... | collective-permute-start | bytes 24584 | tf_op jit(solution)/shard_map/ppermute | solution.py:45
  54.7 0.6 collective-permute-start.20
  55.3 3.4 %collective-permute-start.19 = (f32[24,128]{1,0:T(8,128)S(1)}, f32[24,128]{1,0:T(8,128)S(1)}, u32[]{:S(2)}, u32[]{:S(2)}) collective-permute-start(f32[24,128]{1,0:T(8,128)S(1)} %get-tuple-element.73), channel_id=1, source_target_pairs={{0,5},{1,6},{2,7},{3,0},{4,1},{5,2},{6,3},{7,4},{8,13},{9,14},{10,... | collective-permute-start | bytes 36872 | tf_op jit(solution)/shard_map/ppermute | solution.py:45
  58.7 3.0 %collective-permute-start.25 = (f32[16,128]{1,0:T(8,128)S(1)}, f32[16,128]{1,0:T(8,128)S(1)}, u32[]{:S(2)}, u32[]{:S(2)}) collective-permute-start(f32[16,128]{1,0:T(8,128)S(1)} %add_add_fusion.refs_8_), channel_id=1, source_target_pairs={{0,192},{1,193},{2,194},{3,195},{4,196},{5,197},{6,198},{7,199},{8... | collective-permute-start | bytes 24584 | tf_op jit(solution)/shard_map/ppermute | solution.py:45
  61.7 0.1 collective-permute-start.24
  61.9 0.7 collective-permute-start.23
  62.6 0.3 gather_txt.1.refs_4_.txt_ref
  62.9 2.9 %collective-permute-done.24.refs_10_ = f32[16,128]{1,0:T(8,128)S(1)} collective-permute-done((f32[16,128]{1,0:T(8,128)S(1)}, f32[16,128]{1,0:T(8,128)S(1)}, u32[]{:S(2)}, u32[]{:S(2)}) %collective-permute-start.24) | collective-permute-done | bytes 8224 | tf_op jit(solution)/shard_map/ppermute | solution.py:45
  65.7 2.8 %grad_img.1 = (bf16[528,1280]{1,0:T(8,128)(2,1)S(1)}, bf16[512,1024]{1,0:T(8,128)(2,1)S(1)}, f32[1024,128]{1,0:T(8,128)S(1)}, f32[8,1024]{1,0:T(8,128)S(1)}, f32[8,128]{1,0:T(8,128)S(1)}, /*index=5*/f32[8,128]{1,0:T(8,128)S(1)}) custom-call(s32[16]{0:T(128)S(1)} %get-tuple-element.76.refs_0_, s32[16]{0:T(128)S(1)} %get-tuple-element.77.refs_1_, ...), custom_call_target="tpu_custom_call" | custom-call | flops 1342177280 | bytes 1048576 | tf_op jit(solution)/shard_map/grad_img/pallas_call | solution.py:378
  68.5 4.2 %collective-permute-start.26 = (bf16[528,1280]{1,0:T(8,128)(2,1)S(1)}, bf16[528,1280]{1,0:T(8,128)(2,1)S(1)}, u32[]{:S(2)}, u32[]{:S(2)}) collective-permute-start(bf16[528,1280]{1,0:T(8,128)(2,1)S(1)} %get-tuple-element.47), channel_id=1, source_target_pairs={{0,16},{1,17},{2,18},{3,19},{4,20},{5,21},{6,22},{7,23},{8,24},{9,... | collective-permute-start | bytes 4055048 | tf_op jit(solution)/shard_map/ppermute | solution.py:45
  72.7 3.1 %grad_img_rest.1 = (bf16[528,1280]{1,0:T(8,128)(2,1)S(1)}, bf16[512,1024]{1,0:T(8,128)(2,1)S(1)}) custom-call(f32[4]{0:T(128)S(1)} %pad_maximum_fusion.2.refs_2_.scale_ref, f32[1024,1024]{1,0:T(8,128)S(1)} %get-tuple-element.40.refs_3_.logit_ref, bf16[1024,1280]{1,0:T(8,128)(2,1)S(1)} %gather_txt.1.refs_4_.txt_ref, ...), custom_call_target="tpu_custom_call" | custom-call | flops 1342177280 | bytes 1048576 | tf_op jit(solution)/shard_map/grad_img_rest/pallas_call | solution.py:387
  75.9 0.4 pair.1
  76.2 1.3 %collective-permute-start.27 = (bf16[80,1280]{1,0:T(8,128)(2,1)S(1)}, bf16[80,1280]{1,0:T(8,128)(2,1)S(1)}, u32[]{:S(2)}, u32[]{:S(2)}) collective-permute-start(bf16[80,1280]{1,0:T(8,128)(2,1)S(1)} %get-tuple-element.50), channel_id=1, source_target_pairs={{0,7},{1,0},{2,1},{3,2},{4,3},{5,4},{6,5},{7,6},{8,15},{9,8},{10,9... | collective-permute-start | bytes 614408 | tf_op jit(solution)/shard_map/ppermute | solution.py:45
  77.5 0.9 grad_txt_far.1
  78.4 1.9 %collective-permute-start.30 = (bf16[128,1280]{1,0:T(8,128)(2,1)S(1)}, bf16[128,1280]{1,0:T(8,128)(2,1)S(1)}, u32[]{:S(2)}, u32[]{:S(2)}) collective-permute-start(bf16[128,1280]{1,0:T(8,128)(2,1)S(1)} %get-tuple-element.61), channel_id=1, source_target_pairs={{0,64},{1,65},{2,66},{3,67},{4,68},{5,69},{6,70},{7,71},{8,72},{9,... | collective-permute-start | bytes 983048 | tf_op jit(solution)/shard_map/ppermute | solution.py:45
  80.4 0.8 collective-permute-start.29
  81.2 2.8 %grad_txt.1 = (bf16[256,1280]{1,0:T(8,128)(2,1)S(1)}, bf16[256,1280]{1,0:T(8,128)(2,1)S(1)}, bf16[256,1280]{1,0:T(8,128)(2,1)S(1)}) custom-call(bf16[512,1024]{1,0:T(8,128)(2,1)S(1)} %get-tuple-element.51.low_ref, bf16[512,1024]{1,0:T(8,128)(2,1)S(1)} %get-tuple-element.52.high_ref, bf16[1024,1280]{1,0:T(8,128)(2,1)S(1)} %get-tuple-element.53.img_ref), custom_call_target="tpu_custom_call" | custom-call | flops 2013265920 | bytes 1048576 | tf_op jit(solution)/shard_map/grad_txt/pallas_call | solution.py:410
  84.1 0.1 collective-permute-start.28
  84.2 1.7 %collective-permute-done.30.high_ref = bf16[128,1280]{1,0:T(8,128)(2,1)S(1)} collective-permute-done((bf16[128,1280]{1,0:T(8,128)(2,1)S(1)}, bf16[128,1280]{1,0:T(8,128)(2,1)S(1)}, u32[]{:S(2)}, u32[]{:S(2)}) %collective-permute-start.30) | collective-permute-done | bytes 327712 | tf_op jit(solution)/shard_map/ppermute | solution.py:45
  85.9 1.1 collective-permute-done.29.low_ref
  87.0 0.2 plane_fold.1
  87.2 2.1 %collective-permute-start.35 = (bf16[272,1280]{1,0:T(8,128)(2,1)S(1)}, bf16[272,1280]{1,0:T(8,128)(2,1)S(1)}, u32[]{:S(2)}, u32[]{:S(2)}) collective-permute-start(bf16[272,1280]{1,0:T(8,128)(2,1)S(1)} %get-tuple-element.66), channel_id=1, source_target_pairs={{0,192},{1,193},{2,194},{3,195},{4,196},{5,197},{6,198},{7,199},{8... | collective-permute-start | bytes 2088968 | tf_op jit(solution)/shard_map/ppermute | solution.py:45
  89.3 2.4 %collective-permute-done.28.refs_1_ = bf16[144,1280]{1,0:T(8,128)(2,1)S(1)} collective-permute-done((bf16[144,1280]{1,0:T(8,128)(2,1)S(1)}, bf16[144,1280]{1,0:T(8,128)(2,1)S(1)}, u32[]{:S(2)}, u32[]{:S(2)}) %collective-permute-start.28) | collective-permute-done | bytes 368672 | tf_op jit(solution)/shard_map/ppermute | solution.py:45
  91.7 0.1 ring_fold.3
  91.9 7.9 %collective-permute-done.31.arrived_ref = bf16[144,1280]{1,0:T(8,128)(2,1)S(1)} collective-permute-done((bf16[144,1280]{1,0:T(8,128)(2,1)S(1)}, bf16[144,1280]{1,0:T(8,128)(2,1)S(1)}, u32[]{:S(2)}, u32[]{:S(2)}) %collective-permute-start.31) | collective-permute-done | bytes 368672 | tf_op jit(solution)/shard_map/ppermute | solution.py:45
  99.8 0.1 last_fold.1
  99.9 0.1 collective-permute-start.33
  100.0 0.7 collective-permute-done.36.up_ref
  100.7 0.2 line.1
  101.0 0.4 collective-permute-start.37
  101.4 1.1 collective-permute-start.38
  102.5 1.1 collective-permute-start.39
  103.6 2.2 %collective-permute-done.33.refs_3_ = bf16[80,1280]{1,0:T(8,128)(2,1)S(1)} collective-permute-done((bf16[80,1280]{1,0:T(8,128)(2,1)S(1)}, bf16[80,1280]{1,0:T(8,128)(2,1)S(1)}, u32[]{:S(2)}, u32[]{:S(2)}) %collective-permute-start.33) | collective-permute-done | bytes 204832 | tf_op jit(solution)/shard_map/ppermute | solution.py:45
  105.8 3.8 %collective-permute-start.34 = (bf16[80,1280]{1,0:T(8,128)(2,1)S(1)}, bf16[80,1280]{1,0:T(8,128)(2,1)S(1)}, u32[]{:S(2)}, u32[]{:S(2)}) collective-permute-start(bf16[80,1280]{1,0:T(8,128)(2,1)S(1)} %collective-permute-done.33.refs_3_), channel_id=1, source_target_pairs={{0,16},{1,17},{2,18},{3,19},{4,20},{5,21},{6,22},{7,23},{8,24},{9,... | collective-permute-start | bytes 614408 | tf_op jit(solution)/shard_map/ppermute | solution.py:45
  109.6 5.7 %collective-permute-done.32.refs_1_ = bf16[64,1280]{1,0:T(8,128)(2,1)S(1)} collective-permute-done((bf16[64,1280]{1,0:T(8,128)(2,1)S(1)}, bf16[64,1280]{1,0:T(8,128)(2,1)S(1)}, u32[]{:S(2)}, u32[]{:S(2)}) %collective-permute-start.32) | collective-permute-done | bytes 163872 | tf_op jit(solution)/shard_map/ppermute | solution.py:45
  115.3 1.7 %finish.1 = (bf16[64,1280]{1,0:T(8,128)(2,1)}, bf16[64,1280]{1,0:T(8,128)(2,1)}, f32[1]{0:T(128)}, f32[1]{0:T(128)}) custom-call(f32[4]{0:T(128)S(1)} %pad_maximum_fusion.2.refs_2_.scale_ref, bf16[64,1280]{1,0:T(8,128)(2,1)S(1)} %copy-done.1, bf16[64,1280]{1,0:T(8,128)(2,1)S(1)} %copy-done.3, bf16[64,1280]{1,0:T(8,128)(2,1)S(1)} %normalize_img.1.img_hat_ref.refs_12_, ...), custom_call_target="tpu_custom_call" | custom-call | bytes 1048576 | tf_op jit(solution)/shard_map/finish/pallas_call | solution.py:447
  (58 shorter events, 0.7 us)
Async XLA Ops:
  0.6 0.9 copy-start
  1.7 7.1 %collective-permute-start = (bf16[64,1280]{1,0:T(8,128)(2,1)S(1)}, bf16[64,1280]{1,0:T(8,128)(2,1)S(1)}, u32[]{:S(2)}, u32[]{:S(2)}) collective-permute-start(bf16[64,1280]{1,0:T(8,128)(2,1)S(1)} %normalize_img.1.img_hat_ref.refs_12_), channel_id=1, source_target_pairs={{0,16},{1,17},{2,18},{3,19},{4,20},{5,21},{6,22},{7,23},{8,24},{9,... | collective-permute-start | bytes 491528 | tf_op jit(solution)/shard_map/ppermute | solution.py:45
  5.0 0.9 copy-start.2
  5.9 24.2 %copy-start.4 = (s32[4]{0:T(128)S(1)}, s32[4]{0:T(128)}, u32[]{:S(2)}) copy-start(s32[4]{0:T(128)} %constant.90.clone) | copy-start | bytes 52
  6.1 8.4 %collective-permute-start.4 = (bf16[64,1280]{1,0:T(8,128)(2,1)S(1)}, bf16[64,1280]{1,0:T(8,128)(2,1)S(1)}, u32[]{:S(2)}, u32[]{:S(2)}) collective-permute-start(bf16[64,1280]{1,0:T(8,128)(2,1)S(1)} %normalize_txt.1.txt_hat_ref), channel_id=1, source_target_pairs={{0,32},{1,33},{2,34},{3,35},{4,36},{5,37},{6,38},{7,39},{8,40},{9,... | collective-permute-start | bytes 491528 | tf_op jit(solution)/shard_map/ppermute | solution.py:45
  7.3 7.2 %collective-permute-start.3 = (bf16[64,1280]{1,0:T(8,128)(2,1)S(1)}, bf16[64,1280]{1,0:T(8,128)(2,1)S(1)}, u32[]{:S(2)}, u32[]{:S(2)}) collective-permute-start(bf16[64,1280]{1,0:T(8,128)(2,1)S(1)} %normalize_txt.1.txt_hat_ref), channel_id=1, source_target_pairs={{0,40},{1,41},{2,42},{3,43},{4,44},{5,45},{6,46},{7,47},{8,0},{9,1... | collective-permute-start | bytes 491528 | tf_op jit(solution)/shard_map/ppermute | solution.py:45
  8.1 6.4 %collective-permute-start.2 = (bf16[64,1280]{1,0:T(8,128)(2,1)S(1)}, bf16[64,1280]{1,0:T(8,128)(2,1)S(1)}, u32[]{:S(2)}, u32[]{:S(2)}) collective-permute-start(bf16[64,1280]{1,0:T(8,128)(2,1)S(1)} %normalize_txt.1.txt_hat_ref), channel_id=1, source_target_pairs={{0,8},{1,9},{2,10},{3,11},{4,12},{5,13},{6,14},{7,15},{8,32},{9,33... | collective-permute-start | bytes 491528 | tf_op jit(solution)/shard_map/ppermute | solution.py:45
  8.8 28.7 %copy-start.5 = (s32[16]{0:T(128)S(1)}, s32[16]{0:T(128)}, u32[]{:S(2)}) copy-start(s32[16]{0:T(128)} %constant.92.clone) | copy-start | bytes 196
  8.8 28.7 %copy-start.6 = (s32[16]{0:T(128)S(1)}, s32[16]{0:T(128)}, u32[]{:S(2)}) copy-start(s32[16]{0:T(128)} %constant.91.clone) | copy-start | bytes 196
  8.9 9.7 %collective-permute-start.1 = (bf16[128,1280]{1,0:T(8,128)(2,1)S(1)}, bf16[128,1280]{1,0:T(8,128)(2,1)S(1)}, u32[]{:S(2)}, u32[]{:S(2)}) collective-permute-start(bf16[128,1280]{1,0:T(8,128)(2,1)S(1)} %pad_maximum_fusion.1), channel_id=1, source_target_pairs={{0,1},{1,2},{2,3},{3,4},{4,5},{5,6},{6,7},{7,0},{8,9},{9,10},{10,1... | collective-permute-start | bytes 983048 | tf_op jit(solution)/shard_map/ppermute | solution.py:45
  14.6 15.8 %collective-permute-start.10 = (bf16[256,1280]{1,0:T(8,128)(2,1)S(1)}, bf16[256,1280]{1,0:T(8,128)(2,1)S(1)}, u32[]{:S(2)}, u32[]{:S(2)}) collective-permute-start(bf16[256,1280]{1,0:T(8,128)(2,1)S(1)} %pad_maximum_fusion.refs_13_.refs_0_), channel_id=1, source_target_pairs={{0,192},{1,193},{2,194},{3,195},{4,196},{5,197},{6,198},{7,199},{8... | collective-permute-start | bytes 1966088 | tf_op jit(solution)/shard_map/ppermute | solution.py:45
  17.1 16.0 %collective-permute-start.9 = (bf16[256,1280]{1,0:T(8,128)(2,1)S(1)}, bf16[256,1280]{1,0:T(8,128)(2,1)S(1)}, u32[]{:S(2)}, u32[]{:S(2)}) collective-permute-start(bf16[256,1280]{1,0:T(8,128)(2,1)S(1)} %pad_maximum_fusion.refs_13_.refs_0_), channel_id=1, source_target_pairs={{0,64},{1,65},{2,66},{3,67},{4,68},{5,69},{6,70},{7,71},{8,72},{9,... | collective-permute-start | bytes 1966088 | tf_op jit(solution)/shard_map/ppermute | solution.py:45
  18.5 7.2 %collective-permute-start.6 = (bf16[128,1280]{1,0:T(8,128)(2,1)S(1)}, bf16[128,1280]{1,0:T(8,128)(2,1)S(1)}, u32[]{:S(2)}, u32[]{:S(2)}) collective-permute-start(bf16[128,1280]{1,0:T(8,128)(2,1)S(1)} %collective-permute-done.1.refs_8_), channel_id=1, source_target_pairs={{0,1},{1,2},{2,3},{3,4},{4,5},{5,6},{6,7},{7,0},{8,9},{9,10},{10,1... | collective-permute-start | bytes 983048 | tf_op jit(solution)/shard_map/ppermute | solution.py:45
  25.7 8.2 %collective-permute-start.8 = (bf16[128,1280]{1,0:T(8,128)(2,1)S(1)}, bf16[128,1280]{1,0:T(8,128)(2,1)S(1)}, u32[]{:S(2)}, u32[]{:S(2)}) collective-permute-start(bf16[128,1280]{1,0:T(8,128)(2,1)S(1)} %collective-permute-done.6.refs_9_), channel_id=1, source_target_pairs={{0,1},{1,2},{2,3},{3,4},{4,5},{5,6},{6,7},{7,0},{8,9},{9,10},{10,1... | collective-permute-start | bytes 983048 | tf_op jit(solution)/shard_map/ppermute | solution.py:45
  29.1 7.8 %collective-permute-start.5 = (bf16[128,1280]{1,0:T(8,128)(2,1)S(1)}, bf16[128,1280]{1,0:T(8,128)(2,1)}, u32[]{:S(2)}, u32[]{:S(2)}) collective-permute-start(bf16[128,1280]{1,0:T(8,128)(2,1)S(1)} %collective-permute-done.1.refs_8_), channel_id=1, source_target_pairs={{0,16},{1,17},{2,18},{3,19},{4,20},{5,21},{6,22},{7,23},{8,24},{9,... | collective-permute-start | bytes 983048 | tf_op jit(solution)/shard_map/ppermute | solution.py:45
  30.4 7.2 %collective-permute-start.14 = (bf16[128,1280]{1,0:T(8,128)(2,1)S(1)}, bf16[128,1280]{1,0:T(8,128)(2,1)S(1)}, u32[]{:S(2)}, u32[]{:S(2)}) collective-permute-start(bf16[128,1280]{1,0:T(8,128)(2,1)S(1)} %slice.9), channel_id=1, source_target_pairs={{0,192},{1,193},{2,194},{3,195},{4,196},{5,197},{6,198},{7,199},{8... | collective-permute-start | bytes 983048 | tf_op jit(solution)/shard_map/ppermute | solution.py:45
  33.1 7.5 %collective-permute-start.13 = (bf16[128,1280]{1,0:T(8,128)(2,1)S(1)}, bf16[128,1280]{1,0:T(8,128)(2,1)S(1)}, u32[]{:S(2)}, u32[]{:S(2)}) collective-permute-start(bf16[128,1280]{1,0:T(8,128)(2,1)S(1)} %slice.8), channel_id=1, source_target_pairs={{0,64},{1,65},{2,66},{3,67},{4,68},{5,69},{6,70},{7,71},{8,72},{9,... | collective-permute-start | bytes 983048 | tf_op jit(solution)/shard_map/ppermute | solution.py:45
  33.2 4.4 %collective-permute-start.7 = (bf16[128,1280]{1,0:T(8,128)(2,1)S(1)}, bf16[128,1280]{1,0:T(8,128)(2,1)S(1)}, u32[]{:S(2)}, u32[]{:S(2)}) collective-permute-start(bf16[128,1280]{1,0:T(8,128)(2,1)S(1)} %collective-permute-done.6.refs_9_), channel_id=1, source_target_pairs={{0,16},{1,17},{2,18},{3,19},{4,20},{5,21},{6,22},{7,23},{8,24},{9,... | collective-permute-start | bytes 983048 | tf_op jit(solution)/shard_map/ppermute | solution.py:45
  33.9 7.0 %collective-permute-start.12 = (bf16[128,1280]{1,0:T(8,128)(2,1)S(1)}, bf16[128,1280]{1,0:T(8,128)(2,1)S(1)}, u32[]{:S(2)}, u32[]{:S(2)}) collective-permute-start(bf16[128,1280]{1,0:T(8,128)(2,1)S(1)} %collective-permute-done.8.refs_10_), channel_id=1, source_target_pairs={{0,1},{1,2},{2,3},{3,4},{4,5},{5,6},{6,7},{7,0},{8,9},{9,10},{10,1... | collective-permute-start | bytes 983048 | tf_op jit(solution)/shard_map/ppermute | solution.py:45
  36.9 4.0 %collective-permute-start.11 = (bf16[128,1280]{1,0:T(8,128)(2,1)S(1)}, bf16[128,1280]{1,0:T(8,128)(2,1)S(1)}, u32[]{:S(2)}, u32[]{:S(2)}) collective-permute-start(bf16[128,1280]{1,0:T(8,128)(2,1)S(1)} %collective-permute-done.8.refs_10_), channel_id=1, source_target_pairs={{0,16},{1,17},{2,18},{3,19},{4,20},{5,21},{6,22},{7,23},{8,24},{9,... | collective-permute-start | bytes 983048 | tf_op jit(solution)/shard_map/ppermute | solution.py:45
  45.8 5.8 %collective-permute-start.15 = (f32[24,128]{1,0:T(8,128)S(1)}, f32[24,128]{1,0:T(8,128)S(1)}, u32[]{:S(2)}, u32[]{:S(2)}) collective-permute-start(f32[24,128]{1,0:T(8,128)S(1)} %get-tuple-element.41), channel_id=1, source_target_pairs={{0,16},{1,17},{2,18},{3,19},{4,20},{5,21},{6,22},{7,23},{8,24},{9,... | collective-permute-start | bytes 36872 | tf_op jit(solution)/shard_map/ppermute | solution.py:45
  51.5 3.7 %collective-permute-start.17 = (f32[24,128]{1,0:T(8,128)S(1)}, f32[24,128]{1,0:T(8,128)S(1)}, u32[]{:S(2)}, u32[]{:S(2)}) collective-permute-start(f32[24,128]{1,0:T(8,128)S(1)} %add.94), channel_id=1, source_target_pairs={{0,7},{1,0},{2,1},{3,2},{4,3},{5,4},{6,5},{7,6},{8,15},{9,8},{10,9... | collective-permute-start | bytes 36872 | tf_op jit(solution)/shard_map/ppermute | solution.py:45
  51.5 3.8 %collective-permute-start.16 = (f32[24,128]{1,0:T(8,128)S(1)}, f32[24,128]{1,0:T(8,128)S(1)}, u32[]{:S(2)}, u32[]{:S(2)}) collective-permute-start(f32[24,128]{1,0:T(8,128)S(1)} %add.94), channel_id=1, source_target_pairs={{0,1},{1,2},{2,3},{3,4},{4,5},{5,6},{6,7},{7,0},{8,9},{9,10},{10,1... | collective-permute-start | bytes 36872 | tf_op jit(solution)/shard_map/ppermute | solution.py:45
  53.0 5.7 %collective-permute-start.22 = (f32[16,128]{1,0:T(8,128)S(1)}, f32[16,128]{1,0:T(8,128)S(1)}, u32[]{:S(2)}, u32[]{:S(2)}) collective-permute-start(f32[16,128]{1,0:T(8,128)S(1)} %get-tuple-element.42), channel_id=1, source_target_pairs={{0,40},{1,41},{2,42},{3,43},{4,44},{5,45},{6,46},{7,47},{8,0},{9,1... | collective-permute-start | bytes 24584 | tf_op jit(solution)/shard_map/ppermute | solution.py:45
  54.7 4.0 %collective-permute-start.21 = (f32[16,128]{1,0:T(8,128)S(1)}, f32[16,128]{1,0:T(8,128)S(1)}, u32[]{:S(2)}, u32[]{:S(2)}) collective-permute-start(f32[16,128]{1,0:T(8,128)S(1)} %get-tuple-element.42), channel_id=1, source_target_pairs={{0,32},{1,33},{2,34},{3,35},{4,36},{5,37},{6,38},{7,39},{8,40},{9,... | collective-permute-start | bytes 24584 | tf_op jit(solution)/shard_map/ppermute | solution.py:45
  54.7 4.0 %collective-permute-start.20 = (f32[16,128]{1,0:T(8,128)S(1)}, f32[16,128]{1,0:T(8,128)S(1)}, u32[]{:S(2)}, u32[]{:S(2)}) collective-permute-start(f32[16,128]{1,0:T(8,128)S(1)} %get-tuple-element.42), channel_id=1, source_target_pairs={{0,8},{1,9},{2,10},{3,11},{4,12},{5,13},{6,14},{7,15},{8,32},{9,33... | collective-permute-start | bytes 24584 | tf_op jit(solution)/shard_map/ppermute | solution.py:45
  55.3 10.4 %collective-permute-start.19 = (f32[24,128]{1,0:T(8,128)S(1)}, f32[24,128]{1,0:T(8,128)S(1)}, u32[]{:S(2)}, u32[]{:S(2)}) collective-permute-start(f32[24,128]{1,0:T(8,128)S(1)} %get-tuple-element.73), channel_id=1, source_target_pairs={{0,5},{1,6},{2,7},{3,0},{4,1},{5,2},{6,3},{7,4},{8,13},{9,14},{10,... | collective-permute-start | bytes 36872 | tf_op jit(solution)/shard_map/ppermute | solution.py:45
  58.7 7.1 %collective-permute-start.18 = (f32[24,128]{1,0:T(8,128)S(1)}, f32[24,128]{1,0:T(8,128)S(1)}, u32[]{:S(2)}, u32[]{:S(2)}) collective-permute-start(f32[24,128]{1,0:T(8,128)S(1)} %get-tuple-element.72.refs_5_), channel_id=1, source_target_pairs={{0,3},{1,4},{2,5},{3,6},{4,7},{5,0},{6,1},{7,2},{8,11},{9,12},{10,... | collective-permute-start | bytes 36872 | tf_op jit(solution)/shard_map/ppermute | solution.py:45
  58.7 4.1 %collective-permute-start.25 = (f32[16,128]{1,0:T(8,128)S(1)}, f32[16,128]{1,0:T(8,128)S(1)}, u32[]{:S(2)}, u32[]{:S(2)}) collective-permute-start(f32[16,128]{1,0:T(8,128)S(1)} %add_add_fusion.refs_8_), channel_id=1, source_target_pairs={{0,192},{1,193},{2,194},{3,195},{4,196},{5,197},{6,198},{7,199},{8... | collective-permute-start | bytes 24584 | tf_op jit(solution)/shard_map/ppermute | solution.py:45
  61.7 4.0 %collective-permute-start.24 = (f32[16,128]{1,0:T(8,128)S(1)}, f32[16,128]{1,0:T(8,128)S(1)}, u32[]{:S(2)}, u32[]{:S(2)}) collective-permute-start(f32[16,128]{1,0:T(8,128)S(1)} %add_add_fusion.refs_8_), channel_id=1, source_target_pairs={{0,128},{1,129},{2,130},{3,131},{4,132},{5,133},{6,134},{7,135},{8... | collective-permute-start | bytes 24584 | tf_op jit(solution)/shard_map/ppermute | solution.py:45
  61.9 3.9 %collective-permute-start.23 = (f32[16,128]{1,0:T(8,128)S(1)}, f32[16,128]{1,0:T(8,128)S(1)}, u32[]{:S(2)}, u32[]{:S(2)}) collective-permute-start(f32[16,128]{1,0:T(8,128)S(1)} %add_add_fusion.refs_8_), channel_id=1, source_target_pairs={{0,64},{1,65},{2,66},{3,67},{4,68},{5,69},{6,70},{7,71},{8,72},{9,... | collective-permute-start | bytes 24584 | tf_op jit(solution)/shard_map/ppermute | solution.py:45
  68.5 7.4 %collective-permute-start.26 = (bf16[528,1280]{1,0:T(8,128)(2,1)S(1)}, bf16[528,1280]{1,0:T(8,128)(2,1)S(1)}, u32[]{:S(2)}, u32[]{:S(2)}) collective-permute-start(bf16[528,1280]{1,0:T(8,128)(2,1)S(1)} %get-tuple-element.47), channel_id=1, source_target_pairs={{0,16},{1,17},{2,18},{3,19},{4,20},{5,21},{6,22},{7,23},{8,24},{9,... | collective-permute-start | bytes 4055048 | tf_op jit(solution)/shard_map/ppermute | solution.py:45
  76.2 7.8 %collective-permute-start.27 = (bf16[80,1280]{1,0:T(8,128)(2,1)S(1)}, bf16[80,1280]{1,0:T(8,128)(2,1)S(1)}, u32[]{:S(2)}, u32[]{:S(2)}) collective-permute-start(bf16[80,1280]{1,0:T(8,128)(2,1)S(1)} %get-tuple-element.50), channel_id=1, source_target_pairs={{0,7},{1,0},{2,1},{3,2},{4,3},{5,4},{6,5},{7,6},{8,15},{9,8},{10,9... | collective-permute-start | bytes 614408 | tf_op jit(solution)/shard_map/ppermute | solution.py:45
  78.4 7.5 %collective-permute-start.30 = (bf16[128,1280]{1,0:T(8,128)(2,1)S(1)}, bf16[128,1280]{1,0:T(8,128)(2,1)S(1)}, u32[]{:S(2)}, u32[]{:S(2)}) collective-permute-start(bf16[128,1280]{1,0:T(8,128)(2,1)S(1)} %get-tuple-element.61), channel_id=1, source_target_pairs={{0,64},{1,65},{2,66},{3,67},{4,68},{5,69},{6,70},{7,71},{8,72},{9,... | collective-permute-start | bytes 983048 | tf_op jit(solution)/shard_map/ppermute | solution.py:45
  80.4 6.7 %collective-permute-start.29 = (bf16[144,1280]{1,0:T(8,128)(2,1)S(1)}, bf16[144,1280]{1,0:T(8,128)(2,1)S(1)}, u32[]{:S(2)}, u32[]{:S(2)}) collective-permute-start(bf16[144,1280]{1,0:T(8,128)(2,1)S(1)} %get-tuple-element.60), channel_id=1, source_target_pairs={{0,192},{1,193},{2,194},{3,195},{4,196},{5,197},{6,198},{7,199},{8... | collective-permute-start | bytes 1105928 | tf_op jit(solution)/shard_map/ppermute | solution.py:45
  84.1 7.6 %collective-permute-start.28 = (bf16[144,1280]{1,0:T(8,128)(2,1)S(1)}, bf16[144,1280]{1,0:T(8,128)(2,1)S(1)}, u32[]{:S(2)}, u32[]{:S(2)}) collective-permute-start(bf16[144,1280]{1,0:T(8,128)(2,1)S(1)} %ring_fold.2), channel_id=1, source_target_pairs={{0,7},{1,0},{2,1},{3,2},{4,3},{5,4},{6,5},{7,6},{8,15},{9,8},{10,9... | collective-permute-start | bytes 1105928 | tf_op jit(solution)/shard_map/ppermute | solution.py:45
  87.2 12.8 %collective-permute-start.35 = (bf16[272,1280]{1,0:T(8,128)(2,1)S(1)}, bf16[272,1280]{1,0:T(8,128)(2,1)S(1)}, u32[]{:S(2)}, u32[]{:S(2)}) collective-permute-start(bf16[272,1280]{1,0:T(8,128)(2,1)S(1)} %get-tuple-element.66), channel_id=1, source_target_pairs={{0,192},{1,193},{2,194},{3,195},{4,196},{5,197},{6,198},{7,199},{8... | collective-permute-start | bytes 2088968 | tf_op jit(solution)/shard_map/ppermute | solution.py:45
  89.3 11.4 %collective-permute-start.36 = (bf16[272,1280]{1,0:T(8,128)(2,1)S(1)}, bf16[272,1280]{1,0:T(8,128)(2,1)S(1)}, u32[]{:S(2)}, u32[]{:S(2)}) collective-permute-start(bf16[272,1280]{1,0:T(8,128)(2,1)S(1)} %get-tuple-element.62), channel_id=1, source_target_pairs={{0,64},{1,65},{2,66},{3,67},{4,68},{5,69},{6,70},{7,71},{8,72},{9,... | collective-permute-start | bytes 2088968 | tf_op jit(solution)/shard_map/ppermute | solution.py:45
  91.8 7.9 %collective-permute-start.31 = (bf16[144,1280]{1,0:T(8,128)(2,1)S(1)}, bf16[144,1280]{1,0:T(8,128)(2,1)S(1)}, u32[]{:S(2)}, u32[]{:S(2)}) collective-permute-start(bf16[144,1280]{1,0:T(8,128)(2,1)S(1)} %ring_fold.3), channel_id=1, source_target_pairs={{0,7},{1,0},{2,1},{3,2},{4,3},{5,4},{6,5},{7,6},{8,15},{9,8},{10,9... | collective-permute-start | bytes 1105928 | tf_op jit(solution)/shard_map/ppermute | solution.py:45
  99.9 15.4 %copy-start.1 = (bf16[64,1280]{1,0:T(8,128)(2,1)S(1)}, bf16[64,1280]{1,0:T(8,128)(2,1)}, u32[]{:S(2)}) copy-start(bf16[64,1280]{1,0:T(8,128)(2,1)} %img_ref.1) | copy-start | bytes 491524
  99.9 15.4 %copy-start.3 = (bf16[64,1280]{1,0:T(8,128)(2,1)S(1)}, bf16[64,1280]{1,0:T(8,128)(2,1)}, u32[]{:S(2)}) copy-start(bf16[64,1280]{1,0:T(8,128)(2,1)} %txt_ref.1) | copy-start | bytes 491524
  99.9 5.9 %collective-permute-start.33 = (bf16[80,1280]{1,0:T(8,128)(2,1)S(1)}, bf16[80,1280]{1,0:T(8,128)(2,1)S(1)}, u32[]{:S(2)}, u32[]{:S(2)}) collective-permute-start(bf16[80,1280]{1,0:T(8,128)(2,1)S(1)} %get-tuple-element.65), channel_id=1, source_target_pairs={{0,7},{1,0},{2,1},{3,2},{4,3},{5,4},{6,5},{7,6},{8,15},{9,8},{10,9... | collective-permute-start | bytes 614408 | tf_op jit(solution)/shard_map/ppermute | solution.py:45
  101.0 8.7 %collective-permute-start.37 = (bf16[80,1280]{1,0:T(8,128)(2,1)S(1)}, bf16[80,1280]{1,0:T(8,128)(2,1)S(1)}, u32[]{:S(2)}, u32[]{:S(2)}) collective-permute-start(bf16[80,1280]{1,0:T(8,128)(2,1)S(1)} %get-tuple-element.68), channel_id=1, source_target_pairs={{0,40},{1,41},{2,42},{3,43},{4,44},{5,45},{6,46},{7,47},{8,0},{9,1... | collective-permute-start | bytes 614408 | tf_op jit(solution)/shard_map/ppermute | solution.py:45
  101.4 8.2 %collective-permute-start.38 = (bf16[80,1280]{1,0:T(8,128)(2,1)S(1)}, bf16[80,1280]{1,0:T(8,128)(2,1)S(1)}, u32[]{:S(2)}, u32[]{:S(2)}) collective-permute-start(bf16[80,1280]{1,0:T(8,128)(2,1)S(1)} %get-tuple-element.69), channel_id=1, source_target_pairs={{0,8},{1,9},{2,10},{3,11},{4,12},{5,13},{6,14},{7,15},{8,32},{9,33... | collective-permute-start | bytes 614408 | tf_op jit(solution)/shard_map/ppermute | solution.py:45
  102.5 7.1 %collective-permute-start.39 = (bf16[80,1280]{1,0:T(8,128)(2,1)S(1)}, bf16[80,1280]{1,0:T(8,128)(2,1)S(1)}, u32[]{:S(2)}, u32[]{:S(2)}) collective-permute-start(bf16[80,1280]{1,0:T(8,128)(2,1)S(1)} %get-tuple-element.70), channel_id=1, source_target_pairs={{0,32},{1,33},{2,34},{3,35},{4,36},{5,37},{6,38},{7,39},{8,40},{9,... | collective-permute-start | bytes 614408 | tf_op jit(solution)/shard_map/ppermute | solution.py:45
  105.8 9.5 %collective-permute-start.34 = (bf16[80,1280]{1,0:T(8,128)(2,1)S(1)}, bf16[80,1280]{1,0:T(8,128)(2,1)S(1)}, u32[]{:S(2)}, u32[]{:S(2)}) collective-permute-start(bf16[80,1280]{1,0:T(8,128)(2,1)S(1)} %collective-permute-done.33.refs_3_), channel_id=1, source_target_pairs={{0,16},{1,17},{2,18},{3,19},{4,20},{5,21},{6,22},{7,23},{8,24},{9,... | collective-permute-start | bytes 614408 | tf_op jit(solution)/shard_map/ppermute | solution.py:45
  109.6 5.7 %collective-permute-start.32 = (bf16[64,1280]{1,0:T(8,128)(2,1)S(1)}, bf16[64,1280]{1,0:T(8,128)(2,1)S(1)}, u32[]{:S(2)}, u32[]{:S(2)}) collective-permute-start(bf16[64,1280]{1,0:T(8,128)(2,1)S(1)} %get-tuple-element.64), channel_id=1, source_target_pairs={{0,7},{1,0},{2,1},{3,2},{4,3},{5,4},{6,5},{7,6},{8,15},{9,8},{10,9... | collective-permute-start | bytes 491528 | tf_op jit(solution)/shard_map/ppermute | solution.py:45

commit v2 on v1

--- a/solution.py
+++ b/solution.py
@@ -76,7 +76,11 @@
     hat_ref[...] = unit_rows(raw_ref)[0].astype(BF16)
 
 
-def diagonal_kernel(img_hat_ref, txt_hat_ref, diag_ref):
+def units_kernel(img_raw_ref, txt_raw_ref, img_hat_ref, txt_hat_ref, diag_ref, *outs):
+    for raw_ref, unit_ref, recip_ref in ((img_raw_ref, *outs[:2]), (txt_raw_ref, *outs[2:])):
+        unit, recip = unit_rows(raw_ref)
+        unit_ref[...] = unit
+        recip_ref[...] = jnp.broadcast_to(recip, recip_ref.shape)
     products = img_hat_ref[...].astype(F32) * txt_hat_ref[...].astype(F32)
     diag_ref[...] = jnp.full(diag_ref.shape, jnp.sum(products), F32)
 
@@ -285,18 +289,19 @@
             ref[...] = grad
 
 
-def finish_kernel(scale_ref, img_ref, txt_ref, img_hat_ref, txt_hat_ref, *refs):
+def finish_kernel(scale_ref, img_ref, img_recip, txt_ref, txt_recip, img_hat_ref, txt_hat_ref, *refs):
     own_img, ring_img, sib_img, for_sib, own_txt, txt1, txt2, txt3, col_ref, row_ref = refs[:10]
     grad_img_ref, grad_txt_ref, loss_ref, slope_ref = refs[10:]
     scale = scale_ref[0]
-    for raw, other, parts, out in (
-        (img_ref, txt_hat_ref, (own_img, ring_img, sib_img), grad_img_ref),
-        (txt_ref, img_hat_ref, (own_txt, txt1, txt2, txt3), grad_txt_ref),
+    for unit_ref, recip_ref, other, parts, out in (
+        (img_ref, img_recip, txt_hat_ref, (own_img, ring_img, sib_img), grad_img_ref),
+        (txt_ref, txt_recip, img_hat_ref, (own_txt, txt1, txt2, txt3), grad_txt_ref),
     ):
-        unit, recip = unit_rows(raw)
+        unit = unit_ref[...]
         total = sum(part[0:64, :].astype(F32) for part in parts)
         grad_hat = scale * (total - other[...].astype(F32))
         inner = jnp.sum(grad_hat * unit, axis=1, keepdims=True)
+        recip = jnp.concatenate([recip_ref[...]] * (unit.shape[1] // 128), axis=1)
         out[...] = (recip * (grad_hat - unit * inner)).astype(BF16)
     cols = col_ref[...] + decode(for_sib, 64) + decode(sib_img, 64)
     rows = row_ref[...] + decode(txt1, 64) + decode(txt2, 64) + decode(txt3, 64)
@@ -327,7 +332,10 @@
     total = rows * GROUP
     img_hat = call(normalize_kernel, shape(rows, width), [VMEM], "normalize_img")(image_raw)
     txt_hat = call(normalize_kernel, shape(rows, width), [VMEM], "normalize_txt")(text_raw)
-    diag = call(diagonal_kernel, shape(8, 128, dtype=F32), [VMEM] * 2, "diagonal")(img_hat, txt_hat)
+    unit = (shape(rows, width, dtype=F32), shape(rows, 128, dtype=F32))
+    diag, *units = call(units_kernel, (shape(8, 128, dtype=F32), *unit, *unit), [VMEM] * 4, "units")(
+        image_raw, text_raw, img_hat, txt_hat
+    )
 
     scale = jnp.exp(log_scale[0])
     shift = jnp.maximum(1.01 * scale - 70.0, 0.0)
@@ -447,10 +455,10 @@
     return call(
         finish_kernel,
         (shape(rows, width), shape(rows, width), scalar, scalar),
-        [SMEM] + [VMEM] * 14,
+        [SMEM] + [VMEM] * 16,
         "finish",
         out_specs=(VMEM, VMEM, SMEM, SMEM),
-    )(scales, image_raw, text_raw, img_hat, txt_hat, *img_parts, *txt_parts, col_scalars, row_scalars)
+    )(scales, *units, img_hat, txt_hat, *img_parts, *txt_parts, col_scalars, row_scalars)
 
 
 def solution(mesh):

time: 117 us -> 118 us (level)
  transfers between devices with their start and end apart: 40 -> 40, of which waited for: 13 -> 14; matrix products, arithmetic and copies ran while one was open for 0% -> 0% of each run, Pallas kernels for 7% -> 7%
where the time goes in v2:
time: 118 us
  starting transfers between devices  61.5 us (52%)
  waiting for transfers between devices  34.2 us (29%)
  Pallas kernels  18.1 us (15%)
  local copies, waits for them, and re-layouts  2.06 us (2%)
  between operations  1.79 us (2%)
    ppermute x40, starting transfers between devices, permute(): return lax.ppermute(array, AXES, pairs)  61.5 us
    ppermute x40, waiting for transfers between devices, permute(): return lax.ppermute(array, AXES, pairs)  34.2 us
    pallas_call x1, Pallas kernels, per_device(): call(lambda *refs: logits_kernel(img_order, *refs), (shape(total, width),...  5.07 us
    pallas_call x1, Pallas kernels, per_device(): call(grad_img_rest_kernel, half_grad, [SMEM] + [VMEM] * 5, 'grad_img_rest...  3.14 us
    pallas_call x1, Pallas kernels, per_device(): call(grad_txt_kernel, (shape(256, width),) * 3, [VMEM] * 3, 'grad_txt', f...  2.85 us
    pallas_call x1, Pallas kernels, per_device(): call(grad_img_kernel, half_grad + (shape(total, 128, dtype=F32), shape(8,...  2.77 us
  transfers between devices with their start and end apart: 40, of which 14 were waited for; matrix products, arithmetic and copies ran while one was open for 0% of the time, Pallas kernels for 7%

profile of v2, /device:TPU:1, one launch (start us, length us, event | category | flops | bytes accessed | tf_op | source)
XLA Modules:
  0.0 117.9 jit_solution(4627503552637207178)
XLA Ops:
  0.6 0.9 copy-done
  1.5 0.1 normalize_img.1.img_hat_ref.refs_12_
  1.7 3.3 %collective-permute-start = (bf16[64,1280]{1,0:T(8,128)(2,1)S(1)}, bf16[64,1280]{1,0:T(8,128)(2,1)S(1)}, u32[]{:S(2)}, u32[]{:S(2)}) collective-permute-start(bf16[64,1280]{1,0:T(8,128)(2,1)S(1)} %normalize_img.1.img_hat_ref.refs_12_), channel_id=1, source_target_pairs={{0,16},{1,17},{2,18},{3,19},{4,20},{5,21},{6,22},{7,23},{8,24},{9,... | collective-permute-start | bytes 491528 | tf_op jit(solution)/shard_map/ppermute | solution.py:45
  5.0 0.9 copy-done.2
  5.9 0.1 normalize_txt.1.txt_hat_ref
  6.1 1.3 %collective-permute-start.4 = (bf16[64,1280]{1,0:T(8,128)(2,1)S(1)}, bf16[64,1280]{1,0:T(8,128)(2,1)S(1)}, u32[]{:S(2)}, u32[]{:S(2)}) collective-permute-start(bf16[64,1280]{1,0:T(8,128)(2,1)S(1)} %normalize_txt.1.txt_hat_ref), channel_id=1, source_target_pairs={{0,32},{1,33},{2,34},{3,35},{4,36},{5,37},{6,38},{7,39},{8,40},{9,... | collective-permute-start | bytes 491528 | tf_op jit(solution)/shard_map/ppermute | solution.py:45
  7.3 0.8 collective-permute-start.3
  8.1 0.7 collective-permute-start.2
  8.8 5.7 %collective-permute-start.1 = (bf16[128,1280]{1,0:T(8,128)(2,1)S(1)}, bf16[128,1280]{1,0:T(8,128)(2,1)S(1)}, u32[]{:S(2)}, u32[]{:S(2)}) collective-permute-start(bf16[128,1280]{1,0:T(8,128)(2,1)S(1)} %pad_maximum_fusion.1), channel_id=1, source_target_pairs={{0,1},{1,2},{2,3},{3,4},{4,5},{5,6},{6,7},{7,0},{8,9},{9,10},{10,1... | collective-permute-start | bytes 983048 | tf_op jit(solution)/shard_map/ppermute | solution.py:45
  14.6 2.6 %collective-permute-start.10 = (bf16[256,1280]{1,0:T(8,128)(2,1)S(1)}, bf16[256,1280]{1,0:T(8,128)(2,1)S(1)}, u32[]{:S(2)}, u32[]{:S(2)}) collective-permute-start(bf16[256,1280]{1,0:T(8,128)(2,1)S(1)} %pad_maximum_fusion.refs_13_.refs_0_), channel_id=1, source_target_pairs={{0,192},{1,193},{2,194},{3,195},{4,196},{5,197},{6,198},{7,199},{8... | collective-permute-start | bytes 1966088 | tf_op jit(solution)/shard_map/ppermute | solution.py:45
  17.1 1.4 %collective-permute-done.1.refs_8_ = bf16[128,1280]{1,0:T(8,128)(2,1)S(1)} collective-permute-done((bf16[128,1280]{1,0:T(8,128)(2,1)S(1)}, bf16[128,1280]{1,0:T(8,128)(2,1)S(1)}, u32[]{:S(2)}, u32[]{:S(2)}) %collective-permute-start.1) | collective-permute-done | bytes 327712 | tf_op jit(solution)/shard_map/ppermute | solution.py:45
  18.5 3.2 %collective-permute-start.6 = (bf16[128,1280]{1,0:T(8,128)(2,1)S(1)}, bf16[128,1280]{1,0:T(8,128)(2,1)}, u32[]{:S(2)}, u32[]{:S(2)}) collective-permute-start(bf16[128,1280]{1,0:T(8,128)(2,1)S(1)} %collective-permute-done.1.refs_8_), channel_id=1, source_target_pairs={{0,1},{1,2},{2,3},{3,4},{4,5},{5,6},{6,7},{7,0},{8,9},{9,10},{10,1... | collective-permute-start | bytes 983048 | tf_op jit(solution)/shard_map/ppermute | solution.py:45
  21.7 4.0 %collective-permute-done.6.refs_9_ = bf16[128,1280]{1,0:T(8,128)(2,1)} collective-permute-done((bf16[128,1280]{1,0:T(8,128)(2,1)S(1)}, bf16[128,1280]{1,0:T(8,128)(2,1)}, u32[]{:S(2)}, u32[]{:S(2)}) %collective-permute-start.6) | collective-permute-done | bytes 327712 | tf_op jit(solution)/shard_map/ppermute | solution.py:45
  25.7 3.4 %collective-permute-start.8 = (bf16[128,1280]{1,0:T(8,128)(2,1)}, bf16[128,1280]{1,0:T(8,128)(2,1)}, u32[]{:S(2)}, u32[]{:S(2)}) collective-permute-start(bf16[128,1280]{1,0:T(8,128)(2,1)} %collective-permute-done.6.refs_9_), channel_id=1, source_target_pairs={{0,1},{1,2},{2,3},{3,4},{4,5},{5,6},{6,7},{7,0},{8,9},{9,10},{10,1... | collective-permute-start | bytes 983048 | tf_op jit(solution)/shard_map/ppermute | solution.py:45
  29.1 0.2 collective-permute-start.5
  29.3 0.2 units.1
  30.4 0.1 add.91
  30.5 0.1 add.86
  30.6 2.6 %collective-permute-start.14 = (bf16[128,1280]{1,0:T(8,128)(2,1)S(1)}, bf16[128,1280]{1,0:T(8,128)(2,1)S(1)}, u32[]{:S(2)}, u32[]{:S(2)}) collective-permute-start(bf16[128,1280]{1,0:T(8,128)(2,1)S(1)} %slice.9), channel_id=1, source_target_pairs={{0,192},{1,193},{2,194},{3,195},{4,196},{5,197},{6,198},{7,199},{8... | collective-permute-start | bytes 983048 | tf_op jit(solution)/shard_map/ppermute | solution.py:45
  33.2 0.1 collective-permute-start.13
  33.3 0.8 collective-permute-start.7
  34.1 2.9 %collective-permute-start.12 = (bf16[128,1280]{1,0:T(8,128)(2,1)}, bf16[128,1280]{1,0:T(8,128)(2,1)S(1)}, u32[]{:S(2)}, u32[]{:S(2)}) collective-permute-start(bf16[128,1280]{1,0:T(8,128)(2,1)} %collective-permute-done.8.refs_10_), channel_id=1, source_target_pairs={{0,1},{1,2},{2,3},{3,4},{4,5},{5,6},{6,7},{7,0},{8,9},{9,10},{10,1... | collective-permute-start | bytes 983048 | tf_op jit(solution)/shard_map/ppermute | solution.py:45
  37.0 0.9 collective-permute-start.11
  38.1 2.6 %collective-permute-done.13.refs_16_.refs_3_ = bf16[128,1280]{1,0:T(8,128)(2,1)S(1)} collective-permute-done((bf16[128,1280]{1,0:T(8,128)(2,1)S(1)}, bf16[128,1280]{1,0:T(8,128)(2,1)S(1)}, u32[]{:S(2)}, u32[]{:S(2)}) %collective-permute-start.13) | collective-permute-done | bytes 327712 | tf_op jit(solution)/shard_map/ppermute | solution.py:45
  40.7 0.7 collective-permute-done.12.refs_11_
  41.4 5.1 %logits.1 = (bf16[1024,1280]{1,0:T(8,128)(2,1)S(1)}, f32[1024,1024]{1,0:T(8,128)S(1)}, f32[24,128]{1,0:T(8,128)S(1)}, f32[16,128]{1,0:T(8,128)S(1)}) custom-call(s32[16]{0:T(128)S(1)} %get-tuple-element.86.refs_0_, s32[16]{0:T(128)S(1)} %get-tuple-element.87.refs_1_, f32[4]{0:T(128)S(1)} %pad_maximum_fusion.2.refs_2_.scale_ref, ...), custom_call_target="tpu_custom_call" | custom-call | flops 2684354560 | bytes 1048576 | tf_op jit(solution)/shard_map/logits/pallas_call | solution.py:362
  46.5 5.1 %collective-permute-start.15 = (f32[24,128]{1,0:T(8,128)S(1)}, f32[24,128]{1,0:T(8,128)S(1)}, u32[]{:S(2)}, u32[]{:S(2)}) collective-permute-start(f32[24,128]{1,0:T(8,128)S(1)} %get-tuple-element.51), channel_id=1, source_target_pairs={{0,16},{1,17},{2,18},{3,19},{4,20},{5,21},{6,22},{7,23},{8,24},{9,... | collective-permute-start | bytes 36872 | tf_op jit(solution)/shard_map/ppermute | solution.py:45
  51.6 0.8 collective-permute-done.15
  52.4 1.5 %collective-permute-start.16 = (f32[24,128]{1,0:T(8,128)S(1)}, f32[24,128]{1,0:T(8,128)S(1)}, u32[]{:S(2)}, u32[]{:S(2)}) collective-permute-start(f32[24,128]{1,0:T(8,128)S(1)} %add.94), channel_id=1, source_target_pairs={{0,1},{1,2},{2,3},{3,4},{4,5},{5,6},{6,7},{7,0},{8,9},{9,10},{10,1... | collective-permute-start | bytes 36872 | tf_op jit(solution)/shard_map/ppermute | solution.py:45
  53.9 1.6 %collective-permute-start.22 = (f32[16,128]{1,0:T(8,128)S(1)}, f32[16,128]{1,0:T(8,128)S(1)}, u32[]{:S(2)}, u32[]{:S(2)}) collective-permute-start(f32[16,128]{1,0:T(8,128)S(1)} %get-tuple-element.52), channel_id=1, source_target_pairs={{0,40},{1,41},{2,42},{3,43},{4,44},{5,45},{6,46},{7,47},{8,0},{9,1... | collective-permute-start | bytes 24584 | tf_op jit(solution)/shard_map/ppermute | solution.py:45
  55.5 0.6 collective-permute-start.20
  56.2 3.4 %collective-permute-start.19 = (f32[24,128]{1,0:T(8,128)S(1)}, f32[24,128]{1,0:T(8,128)S(1)}, u32[]{:S(2)}, u32[]{:S(2)}) collective-permute-start(f32[24,128]{1,0:T(8,128)S(1)} %get-tuple-element.83), channel_id=1, source_target_pairs={{0,5},{1,6},{2,7},{3,0},{4,1},{5,2},{6,3},{7,4},{8,13},{9,14},{10,... | collective-permute-start | bytes 36872 | tf_op jit(solution)/shard_map/ppermute | solution.py:45
  59.6 3.0 %collective-permute-start.25 = (f32[16,128]{1,0:T(8,128)S(1)}, f32[16,128]{1,0:T(8,128)S(1)}, u32[]{:S(2)}, u32[]{:S(2)}) collective-permute-start(f32[16,128]{1,0:T(8,128)S(1)} %add_add_fusion.refs_8_), channel_id=1, source_target_pairs={{0,192},{1,193},{2,194},{3,195},{4,196},{5,197},{6,198},{7,199},{8... | collective-permute-start | bytes 24584 | tf_op jit(solution)/shard_map/ppermute | solution.py:45
  62.6 0.1 collective-permute-start.24
  62.7 0.7 collective-permute-start.23
  63.4 0.3 gather_txt.1.refs_4_.txt_ref
  63.7 2.9 %collective-permute-done.24.refs_10_ = f32[16,128]{1,0:T(8,128)S(1)} collective-permute-done((f32[16,128]{1,0:T(8,128)S(1)}, f32[16,128]{1,0:T(8,128)S(1)}, u32[]{:S(2)}, u32[]{:S(2)}) %collective-permute-start.24) | collective-permute-done | bytes 8224 | tf_op jit(solution)/shard_map/ppermute | solution.py:45
  66.6 2.8 %grad_img.1 = (bf16[528,1280]{1,0:T(8,128)(2,1)S(1)}, bf16[512,1024]{1,0:T(8,128)(2,1)S(1)}, f32[1024,128]{1,0:T(8,128)S(1)}, f32[8,1024]{1,0:T(8,128)S(1)}, f32[8,128]{1,0:T(8,128)S(1)}, /*index=5*/f32[8,128]{1,0:T(8,128)S(1)}) custom-call(s32[16]{0:T(128)S(1)} %get-tuple-element.86.refs_0_, s32[16]{0:T(128)S(1)} %get-tuple-element.87.refs_1_, ...), custom_call_target="tpu_custom_call" | custom-call | flops 1342177280 | bytes 1048576 | tf_op jit(solution)/shard_map/grad_img/pallas_call | solution.py:386
  69.4 4.2 %collective-permute-start.26 = (bf16[528,1280]{1,0:T(8,128)(2,1)S(1)}, bf16[528,1280]{1,0:T(8,128)(2,1)S(1)}, u32[]{:S(2)}, u32[]{:S(2)}) collective-permute-start(bf16[528,1280]{1,0:T(8,128)(2,1)S(1)} %get-tuple-element.57), channel_id=1, source_target_pairs={{0,16},{1,17},{2,18},{3,19},{4,20},{5,21},{6,22},{7,23},{8,24},{9,... | collective-permute-start | bytes 4055048 | tf_op jit(solution)/shard_map/ppermute | solution.py:45
  73.5 3.1 %grad_img_rest.1 = (bf16[528,1280]{1,0:T(8,128)(2,1)S(1)}, bf16[512,1024]{1,0:T(8,128)(2,1)S(1)}) custom-call(f32[4]{0:T(128)S(1)} %pad_maximum_fusion.2.refs_2_.scale_ref, f32[1024,1024]{1,0:T(8,128)S(1)} %get-tuple-element.50.refs_3_.logit_ref, bf16[1024,1280]{1,0:T(8,128)(2,1)S(1)} %gather_txt.1.refs_4_.txt_ref, ...), custom_call_target="tpu_custom_call" | custom-call | flops 1342177280 | bytes 1048576 | tf_op jit(solution)/shard_map/grad_img_rest/pallas_call | solution.py:395
  76.7 0.4 pair.1
  77.1 1.3 %collective-permute-start.27 = (bf16[80,1280]{1,0:T(8,128)(2,1)S(1)}, bf16[80,1280]{1,0:T(8,128)(2,1)S(1)}, u32[]{:S(2)}, u32[]{:S(2)}) collective-permute-start(bf16[80,1280]{1,0:T(8,128)(2,1)S(1)} %get-tuple-element.60), channel_id=1, source_target_pairs={{0,7},{1,0},{2,1},{3,2},{4,3},{5,4},{6,5},{7,6},{8,15},{9,8},{10,9... | collective-permute-start | bytes 614408 | tf_op jit(solution)/shard_map/ppermute | solution.py:45
  78.4 0.9 grad_txt_far.1
  79.3 1.9 %collective-permute-start.30 = (bf16[128,1280]{1,0:T(8,128)(2,1)S(1)}, bf16[128,1280]{1,0:T(8,128)(2,1)S(1)}, u32[]{:S(2)}, u32[]{:S(2)}) collective-permute-start(bf16[128,1280]{1,0:T(8,128)(2,1)S(1)} %get-tuple-element.71), channel_id=1, source_target_pairs={{0,64},{1,65},{2,66},{3,67},{4,68},{5,69},{6,70},{7,71},{8,72},{9,... | collective-permute-start | bytes 983048 | tf_op jit(solution)/shard_map/ppermute | solution.py:45
  81.2 0.8 collective-permute-start.29
  82.0 2.8 %grad_txt.1 = (bf16[256,1280]{1,0:T(8,128)(2,1)S(1)}, bf16[256,1280]{1,0:T(8,128)(2,1)S(1)}, bf16[256,1280]{1,0:T(8,128)(2,1)S(1)}) custom-call(bf16[512,1024]{1,0:T(8,128)(2,1)S(1)} %get-tuple-element.61.low_ref, bf16[512,1024]{1,0:T(8,128)(2,1)S(1)} %get-tuple-element.62.high_ref, bf16[1024,1280]{1,0:T(8,128)(2,1)S(1)} %get-tuple-element.63.img_ref), custom_call_target="tpu_custom_call" | custom-call | flops 2013265920 | bytes 1048576 | tf_op jit(solution)/shard_map/grad_txt/pallas_call | solution.py:418
  85.0 0.1 collective-permute-start.28
  85.1 1.7 %collective-permute-done.30.high_ref = bf16[128,1280]{1,0:T(8,128)(2,1)S(1)} collective-permute-done((bf16[128,1280]{1,0:T(8,128)(2,1)S(1)}, bf16[128,1280]{1,0:T(8,128)(2,1)S(1)}, u32[]{:S(2)}, u32[]{:S(2)}) %collective-permute-start.30) | collective-permute-done | bytes 327712 | tf_op jit(solution)/shard_map/ppermute | solution.py:45
  86.8 1.1 collective-permute-done.29.low_ref
  87.8 0.2 plane_fold.1
  88.0 2.1 %collective-permute-start.35 = (bf16[272,1280]{1,0:T(8,128)(2,1)S(1)}, bf16[272,1280]{1,0:T(8,128)(2,1)S(1)}, u32[]{:S(2)}, u32[]{:S(2)}) collective-permute-start(bf16[272,1280]{1,0:T(8,128)(2,1)S(1)} %get-tuple-element.76), channel_id=1, source_target_pairs={{0,192},{1,193},{2,194},{3,195},{4,196},{5,197},{6,198},{7,199},{8... | collective-permute-start | bytes 2088968 | tf_op jit(solution)/shard_map/ppermute | solution.py:45
  90.2 2.4 %collective-permute-done.28.refs_1_ = bf16[144,1280]{1,0:T(8,128)(2,1)S(1)} collective-permute-done((bf16[144,1280]{1,0:T(8,128)(2,1)S(1)}, bf16[144,1280]{1,0:T(8,128)(2,1)S(1)}, u32[]{:S(2)}, u32[]{:S(2)}) %collective-permute-start.28) | collective-permute-done | bytes 368672 | tf_op jit(solution)/shard_map/ppermute | solution.py:45
  92.6 0.1 ring_fold.3
  92.8 7.9 %collective-permute-done.31.arrived_ref = bf16[144,1280]{1,0:T(8,128)(2,1)S(1)} collective-permute-done((bf16[144,1280]{1,0:T(8,128)(2,1)S(1)}, bf16[144,1280]{1,0:T(8,128)(2,1)S(1)}, u32[]{:S(2)}, u32[]{:S(2)}) %collective-permute-start.31) | collective-permute-done | bytes 368672 | tf_op jit(solution)/shard_map/ppermute | solution.py:45
  100.7 0.1 last_fold.1
  100.8 0.7 collective-permute-done.36.up_ref
  101.6 0.2 line.1
  101.8 0.4 collective-permute-start.37
  102.2 1.1 collective-permute-start.38
  103.4 1.1 collective-permute-start.39
  104.5 2.1 %collective-permute-done.33.refs_3_ = bf16[80,1280]{1,0:T(8,128)(2,1)S(1)} collective-permute-done((bf16[80,1280]{1,0:T(8,128)(2,1)S(1)}, bf16[80,1280]{1,0:T(8,128)(2,1)S(1)}, u32[]{:S(2)}, u32[]{:S(2)}) %collective-permute-start.33) | collective-permute-done | bytes 204832 | tf_op jit(solution)/shard_map/ppermute | solution.py:45
  106.6 3.8 %collective-permute-start.34 = (bf16[80,1280]{1,0:T(8,128)(2,1)S(1)}, bf16[80,1280]{1,0:T(8,128)(2,1)S(1)}, u32[]{:S(2)}, u32[]{:S(2)}) collective-permute-start(bf16[80,1280]{1,0:T(8,128)(2,1)S(1)} %collective-permute-done.33.refs_3_), channel_id=1, source_target_pairs={{0,16},{1,17},{2,18},{3,19},{4,20},{5,21},{6,22},{7,23},{8,24},{9,... | collective-permute-start | bytes 614408 | tf_op jit(solution)/shard_map/ppermute | solution.py:45
  110.5 5.7 %collective-permute-done.32.refs_1_ = bf16[64,1280]{1,0:T(8,128)(2,1)S(1)} collective-permute-done((bf16[64,1280]{1,0:T(8,128)(2,1)S(1)}, bf16[64,1280]{1,0:T(8,128)(2,1)S(1)}, u32[]{:S(2)}, u32[]{:S(2)}) %collective-permute-start.32) | collective-permute-done | bytes 163872 | tf_op jit(solution)/shard_map/ppermute | solution.py:45
  116.2 1.6 %finish.1 = (bf16[64,1280]{1,0:T(8,128)(2,1)}, bf16[64,1280]{1,0:T(8,128)(2,1)}, f32[1]{0:T(128)}, f32[1]{0:T(128)}) custom-call(f32[4]{0:T(128)S(1)} %pad_maximum_fusion.2.refs_2_.scale_ref, f32[64,1280]{1,0:T(8,128)S(1)} %get-tuple-element.43.img_ref, f32[64,128]{1,0:T(8,128)S(1)} %get-tuple-element.44.img_recip, ...), custom_call_target="tpu_custom_call" | custom-call | bytes 1048576 | tf_op jit(solution)/shard_map/finish/pallas_call | solution.py:455
  (56 shorter events, 0.7 us)
Async XLA Ops:
  0.6 0.9 copy-start
  1.5 27.8 %copy-start.1 = (bf16[64,1280]{1,0:T(8,128)(2,1)S(1)}, bf16[64,1280]{1,0:T(8,128)(2,1)}, u32[]{:S(2)}) copy-start(bf16[64,1280]{1,0:T(8,128)(2,1)} %img_raw_ref.1) | copy-start | bytes 491524
  1.7 7.1 %collective-permute-start = (bf16[64,1280]{1,0:T(8,128)(2,1)S(1)}, bf16[64,1280]{1,0:T(8,128)(2,1)S(1)}, u32[]{:S(2)}, u32[]{:S(2)}) collective-permute-start(bf16[64,1280]{1,0:T(8,128)(2,1)S(1)} %normalize_img.1.img_hat_ref.refs_12_), channel_id=1, source_target_pairs={{0,16},{1,17},{2,18},{3,19},{4,20},{5,21},{6,22},{7,23},{8,24},{9,... | collective-permute-start | bytes 491528 | tf_op jit(solution)/shard_map/ppermute | solution.py:45
  5.0 0.9 copy-start.2
  6.1 24.2 %copy-start.3 = (s32[4]{0:T(128)S(1)}, s32[4]{0:T(128)}, u32[]{:S(2)}) copy-start(s32[4]{0:T(128)} %constant.90.clone) | copy-start | bytes 52
  6.1 8.4 %collective-permute-start.4 = (bf16[64,1280]{1,0:T(8,128)(2,1)S(1)}, bf16[64,1280]{1,0:T(8,128)(2,1)S(1)}, u32[]{:S(2)}, u32[]{:S(2)}) collective-permute-start(bf16[64,1280]{1,0:T(8,128)(2,1)S(1)} %normalize_txt.1.txt_hat_ref), channel_id=1, source_target_pairs={{0,32},{1,33},{2,34},{3,35},{4,36},{5,37},{6,38},{7,39},{8,40},{9,... | collective-permute-start | bytes 491528 | tf_op jit(solution)/shard_map/ppermute | solution.py:45
  7.3 7.2 %collective-permute-start.3 = (bf16[64,1280]{1,0:T(8,128)(2,1)S(1)}, bf16[64,1280]{1,0:T(8,128)(2,1)S(1)}, u32[]{:S(2)}, u32[]{:S(2)}) collective-permute-start(bf16[64,1280]{1,0:T(8,128)(2,1)S(1)} %normalize_txt.1.txt_hat_ref), channel_id=1, source_target_pairs={{0,40},{1,41},{2,42},{3,43},{4,44},{5,45},{6,46},{7,47},{8,0},{9,1... | collective-permute-start | bytes 491528 | tf_op jit(solution)/shard_map/ppermute | solution.py:45
  8.1 6.4 %collective-permute-start.2 = (bf16[64,1280]{1,0:T(8,128)(2,1)S(1)}, bf16[64,1280]{1,0:T(8,128)(2,1)S(1)}, u32[]{:S(2)}, u32[]{:S(2)}) collective-permute-start(bf16[64,1280]{1,0:T(8,128)(2,1)S(1)} %normalize_txt.1.txt_hat_ref), channel_id=1, source_target_pairs={{0,8},{1,9},{2,10},{3,11},{4,12},{5,13},{6,14},{7,15},{8,32},{9,33... | collective-permute-start | bytes 491528 | tf_op jit(solution)/shard_map/ppermute | solution.py:45
  8.8 9.7 %collective-permute-start.1 = (bf16[128,1280]{1,0:T(8,128)(2,1)S(1)}, bf16[128,1280]{1,0:T(8,128)(2,1)S(1)}, u32[]{:S(2)}, u32[]{:S(2)}) collective-permute-start(bf16[128,1280]{1,0:T(8,128)(2,1)S(1)} %pad_maximum_fusion.1), channel_id=1, source_target_pairs={{0,1},{1,2},{2,3},{3,4},{4,5},{5,6},{6,7},{7,0},{8,9},{9,10},{10,1... | collective-permute-start | bytes 983048 | tf_op jit(solution)/shard_map/ppermute | solution.py:45
  14.6 23.5 %copy-start.4 = (s32[16]{0:T(128)S(1)}, s32[16]{0:T(128)}, u32[]{:S(2)}) copy-start(s32[16]{0:T(128)} %constant.92.clone) | copy-start | bytes 196
  14.6 23.4 %copy-start.5 = (s32[16]{0:T(128)S(1)}, s32[16]{0:T(128)}, u32[]{:S(2)}) copy-start(s32[16]{0:T(128)} %constant.91.clone) | copy-start | bytes 196
  14.6 16.0 %collective-permute-start.10 = (bf16[256,1280]{1,0:T(8,128)(2,1)S(1)}, bf16[256,1280]{1,0:T(8,128)(2,1)S(1)}, u32[]{:S(2)}, u32[]{:S(2)}) collective-permute-start(bf16[256,1280]{1,0:T(8,128)(2,1)S(1)} %pad_maximum_fusion.refs_13_.refs_0_), channel_id=1, source_target_pairs={{0,192},{1,193},{2,194},{3,195},{4,196},{5,197},{6,198},{7,199},{8... | collective-permute-start | bytes 1966088 | tf_op jit(solution)/shard_map/ppermute | solution.py:45
  17.1 16.0 %collective-permute-start.9 = (bf16[256,1280]{1,0:T(8,128)(2,1)S(1)}, bf16[256,1280]{1,0:T(8,128)(2,1)S(1)}, u32[]{:S(2)}, u32[]{:S(2)}) collective-permute-start(bf16[256,1280]{1,0:T(8,128)(2,1)S(1)} %pad_maximum_fusion.refs_13_.refs_0_), channel_id=1, source_target_pairs={{0,64},{1,65},{2,66},{3,67},{4,68},{5,69},{6,70},{7,71},{8,72},{9,... | collective-permute-start | bytes 1966088 | tf_op jit(solution)/shard_map/ppermute | solution.py:45
  18.5 7.2 %collective-permute-start.6 = (bf16[128,1280]{1,0:T(8,128)(2,1)S(1)}, bf16[128,1280]{1,0:T(8,128)(2,1)}, u32[]{:S(2)}, u32[]{:S(2)}) collective-permute-start(bf16[128,1280]{1,0:T(8,128)(2,1)S(1)} %collective-permute-done.1.refs_8_), channel_id=1, source_target_pairs={{0,1},{1,2},{2,3},{3,4},{4,5},{5,6},{6,7},{7,0},{8,9},{9,10},{10,1... | collective-permute-start | bytes 983048 | tf_op jit(solution)/shard_map/ppermute | solution.py:45
  25.7 8.4 %collective-permute-start.8 = (bf16[128,1280]{1,0:T(8,128)(2,1)}, bf16[128,1280]{1,0:T(8,128)(2,1)}, u32[]{:S(2)}, u32[]{:S(2)}) collective-permute-start(bf16[128,1280]{1,0:T(8,128)(2,1)} %collective-permute-done.6.refs_9_), channel_id=1, source_target_pairs={{0,1},{1,2},{2,3},{3,4},{4,5},{5,6},{6,7},{7,0},{8,9},{9,10},{10,1... | collective-permute-start | bytes 983048 | tf_op jit(solution)/shard_map/ppermute | solution.py:45
  29.1 7.9 %collective-permute-start.5 = (bf16[128,1280]{1,0:T(8,128)(2,1)S(1)}, bf16[128,1280]{1,0:T(8,128)(2,1)}, u32[]{:S(2)}, u32[]{:S(2)}) collective-permute-start(bf16[128,1280]{1,0:T(8,128)(2,1)S(1)} %collective-permute-done.1.refs_8_), channel_id=1, source_target_pairs={{0,16},{1,17},{2,18},{3,19},{4,20},{5,21},{6,22},{7,23},{8,24},{9,... | collective-permute-start | bytes 983048 | tf_op jit(solution)/shard_map/ppermute | solution.py:45
  30.6 7.5 %collective-permute-start.14 = (bf16[128,1280]{1,0:T(8,128)(2,1)S(1)}, bf16[128,1280]{1,0:T(8,128)(2,1)S(1)}, u32[]{:S(2)}, u32[]{:S(2)}) collective-permute-start(bf16[128,1280]{1,0:T(8,128)(2,1)S(1)} %slice.9), channel_id=1, source_target_pairs={{0,192},{1,193},{2,194},{3,195},{4,196},{5,197},{6,198},{7,199},{8... | collective-permute-start | bytes 983048 | tf_op jit(solution)/shard_map/ppermute | solution.py:45
  33.2 7.5 %collective-permute-start.13 = (bf16[128,1280]{1,0:T(8,128)(2,1)S(1)}, bf16[128,1280]{1,0:T(8,128)(2,1)S(1)}, u32[]{:S(2)}, u32[]{:S(2)}) collective-permute-start(bf16[128,1280]{1,0:T(8,128)(2,1)S(1)} %slice.8), channel_id=1, source_target_pairs={{0,64},{1,65},{2,66},{3,67},{4,68},{5,69},{6,70},{7,71},{8,72},{9,... | collective-permute-start | bytes 983048 | tf_op jit(solution)/shard_map/ppermute | solution.py:45
  33.3 4.8 %collective-permute-start.7 = (bf16[128,1280]{1,0:T(8,128)(2,1)}, bf16[128,1280]{1,0:T(8,128)(2,1)S(1)}, u32[]{:S(2)}, u32[]{:S(2)}) collective-permute-start(bf16[128,1280]{1,0:T(8,128)(2,1)} %collective-permute-done.6.refs_9_), channel_id=1, source_target_pairs={{0,16},{1,17},{2,18},{3,19},{4,20},{5,21},{6,22},{7,23},{8,24},{9,... | collective-permute-start | bytes 983048 | tf_op jit(solution)/shard_map/ppermute | solution.py:45
  34.1 7.3 %collective-permute-start.12 = (bf16[128,1280]{1,0:T(8,128)(2,1)}, bf16[128,1280]{1,0:T(8,128)(2,1)S(1)}, u32[]{:S(2)}, u32[]{:S(2)}) collective-permute-start(bf16[128,1280]{1,0:T(8,128)(2,1)} %collective-permute-done.8.refs_10_), channel_id=1, source_target_pairs={{0,1},{1,2},{2,3},{3,4},{4,5},{5,6},{6,7},{7,0},{8,9},{9,10},{10,1... | collective-permute-start | bytes 983048 | tf_op jit(solution)/shard_map/ppermute | solution.py:45
  37.0 4.3 %collective-permute-start.11 = (bf16[128,1280]{1,0:T(8,128)(2,1)}, bf16[128,1280]{1,0:T(8,128)(2,1)S(1)}, u32[]{:S(2)}, u32[]{:S(2)}) collective-permute-start(bf16[128,1280]{1,0:T(8,128)(2,1)} %collective-permute-done.8.refs_10_), channel_id=1, source_target_pairs={{0,16},{1,17},{2,18},{3,19},{4,20},{5,21},{6,22},{7,23},{8,24},{9,... | collective-permute-start | bytes 983048 | tf_op jit(solution)/shard_map/ppermute | solution.py:45
  46.5 5.9 %collective-permute-start.15 = (f32[24,128]{1,0:T(8,128)S(1)}, f32[24,128]{1,0:T(8,128)S(1)}, u32[]{:S(2)}, u32[]{:S(2)}) collective-permute-start(f32[24,128]{1,0:T(8,128)S(1)} %get-tuple-element.51), channel_id=1, source_target_pairs={{0,16},{1,17},{2,18},{3,19},{4,20},{5,21},{6,22},{7,23},{8,24},{9,... | collective-permute-start | bytes 36872 | tf_op jit(solution)/shard_map/ppermute | solution.py:45
  52.4 3.7 %collective-permute-start.17 = (f32[24,128]{1,0:T(8,128)S(1)}, f32[24,128]{1,0:T(8,128)S(1)}, u32[]{:S(2)}, u32[]{:S(2)}) collective-permute-start(f32[24,128]{1,0:T(8,128)S(1)} %add.94), channel_id=1, source_target_pairs={{0,7},{1,0},{2,1},{3,2},{4,3},{5,4},{6,5},{7,6},{8,15},{9,8},{10,9... | collective-permute-start | bytes 36872 | tf_op jit(solution)/shard_map/ppermute | solution.py:45
  52.4 3.8 %collective-permute-start.16 = (f32[24,128]{1,0:T(8,128)S(1)}, f32[24,128]{1,0:T(8,128)S(1)}, u32[]{:S(2)}, u32[]{:S(2)}) collective-permute-start(f32[24,128]{1,0:T(8,128)S(1)} %add.94), channel_id=1, source_target_pairs={{0,1},{1,2},{2,3},{3,4},{4,5},{5,6},{6,7},{7,0},{8,9},{9,10},{10,1... | collective-permute-start | bytes 36872 | tf_op jit(solution)/shard_map/ppermute | solution.py:45
  53.9 5.7 %collective-permute-start.22 = (f32[16,128]{1,0:T(8,128)S(1)}, f32[16,128]{1,0:T(8,128)S(1)}, u32[]{:S(2)}, u32[]{:S(2)}) collective-permute-start(f32[16,128]{1,0:T(8,128)S(1)} %get-tuple-element.52), channel_id=1, source_target_pairs={{0,40},{1,41},{2,42},{3,43},{4,44},{5,45},{6,46},{7,47},{8,0},{9,1... | collective-permute-start | bytes 24584 | tf_op jit(solution)/shard_map/ppermute | solution.py:45
  55.5 4.0 %collective-permute-start.21 = (f32[16,128]{1,0:T(8,128)S(1)}, f32[16,128]{1,0:T(8,128)S(1)}, u32[]{:S(2)}, u32[]{:S(2)}) collective-permute-start(f32[16,128]{1,0:T(8,128)S(1)} %get-tuple-element.52), channel_id=1, source_target_pairs={{0,32},{1,33},{2,34},{3,35},{4,36},{5,37},{6,38},{7,39},{8,40},{9,... | collective-permute-start | bytes 24584 | tf_op jit(solution)/shard_map/ppermute | solution.py:45
  55.5 4.0 %collective-permute-start.20 = (f32[16,128]{1,0:T(8,128)S(1)}, f32[16,128]{1,0:T(8,128)S(1)}, u32[]{:S(2)}, u32[]{:S(2)}) collective-permute-start(f32[16,128]{1,0:T(8,128)S(1)} %get-tuple-element.52), channel_id=1, source_target_pairs={{0,8},{1,9},{2,10},{3,11},{4,12},{5,13},{6,14},{7,15},{8,32},{9,33... | collective-permute-start | bytes 24584 | tf_op jit(solution)/shard_map/ppermute | solution.py:45
  56.2 10.4 %collective-permute-start.19 = (f32[24,128]{1,0:T(8,128)S(1)}, f32[24,128]{1,0:T(8,128)S(1)}, u32[]{:S(2)}, u32[]{:S(2)}) collective-permute-start(f32[24,128]{1,0:T(8,128)S(1)} %get-tuple-element.83), channel_id=1, source_target_pairs={{0,5},{1,6},{2,7},{3,0},{4,1},{5,2},{6,3},{7,4},{8,13},{9,14},{10,... | collective-permute-start | bytes 36872 | tf_op jit(solution)/shard_map/ppermute | solution.py:45
  59.5 7.1 %collective-permute-start.18 = (f32[24,128]{1,0:T(8,128)S(1)}, f32[24,128]{1,0:T(8,128)S(1)}, u32[]{:S(2)}, u32[]{:S(2)}) collective-permute-start(f32[24,128]{1,0:T(8,128)S(1)} %get-tuple-element.82.refs_5_), channel_id=1, source_target_pairs={{0,3},{1,4},{2,5},{3,6},{4,7},{5,0},{6,1},{7,2},{8,11},{9,12},{10,... | collective-permute-start | bytes 36872 | tf_op jit(solution)/shard_map/ppermute | solution.py:45
  59.6 4.1 %collective-permute-start.25 = (f32[16,128]{1,0:T(8,128)S(1)}, f32[16,128]{1,0:T(8,128)S(1)}, u32[]{:S(2)}, u32[]{:S(2)}) collective-permute-start(f32[16,128]{1,0:T(8,128)S(1)} %add_add_fusion.refs_8_), channel_id=1, source_target_pairs={{0,192},{1,193},{2,194},{3,195},{4,196},{5,197},{6,198},{7,199},{8... | collective-permute-start | bytes 24584 | tf_op jit(solution)/shard_map/ppermute | solution.py:45
  62.6 4.0 %collective-permute-start.24 = (f32[16,128]{1,0:T(8,128)S(1)}, f32[16,128]{1,0:T(8,128)S(1)}, u32[]{:S(2)}, u32[]{:S(2)}) collective-permute-start(f32[16,128]{1,0:T(8,128)S(1)} %add_add_fusion.refs_8_), channel_id=1, source_target_pairs={{0,128},{1,129},{2,130},{3,131},{4,132},{5,133},{6,134},{7,135},{8... | collective-permute-start | bytes 24584 | tf_op jit(solution)/shard_map/ppermute | solution.py:45
  62.7 3.9 %collective-permute-start.23 = (f32[16,128]{1,0:T(8,128)S(1)}, f32[16,128]{1,0:T(8,128)S(1)}, u32[]{:S(2)}, u32[]{:S(2)}) collective-permute-start(f32[16,128]{1,0:T(8,128)S(1)} %add_add_fusion.refs_8_), channel_id=1, source_target_pairs={{0,64},{1,65},{2,66},{3,67},{4,68},{5,69},{6,70},{7,71},{8,72},{9,... | collective-permute-start | bytes 24584 | tf_op jit(solution)/shard_map/ppermute | solution.py:45
  69.4 7.3 %collective-permute-start.26 = (bf16[528,1280]{1,0:T(8,128)(2,1)S(1)}, bf16[528,1280]{1,0:T(8,128)(2,1)S(1)}, u32[]{:S(2)}, u32[]{:S(2)}) collective-permute-start(bf16[528,1280]{1,0:T(8,128)(2,1)S(1)} %get-tuple-element.57), channel_id=1, source_target_pairs={{0,16},{1,17},{2,18},{3,19},{4,20},{5,21},{6,22},{7,23},{8,24},{9,... | collective-permute-start | bytes 4055048 | tf_op jit(solution)/shard_map/ppermute | solution.py:45
  77.1 7.8 %collective-permute-start.27 = (bf16[80,1280]{1,0:T(8,128)(2,1)S(1)}, bf16[80,1280]{1,0:T(8,128)(2,1)S(1)}, u32[]{:S(2)}, u32[]{:S(2)}) collective-permute-start(bf16[80,1280]{1,0:T(8,128)(2,1)S(1)} %get-tuple-element.60), channel_id=1, source_target_pairs={{0,7},{1,0},{2,1},{3,2},{4,3},{5,4},{6,5},{7,6},{8,15},{9,8},{10,9... | collective-permute-start | bytes 614408 | tf_op jit(solution)/shard_map/ppermute | solution.py:45
  79.3 7.5 %collective-permute-start.30 = (bf16[128,1280]{1,0:T(8,128)(2,1)S(1)}, bf16[128,1280]{1,0:T(8,128)(2,1)S(1)}, u32[]{:S(2)}, u32[]{:S(2)}) collective-permute-start(bf16[128,1280]{1,0:T(8,128)(2,1)S(1)} %get-tuple-element.71), channel_id=1, source_target_pairs={{0,64},{1,65},{2,66},{3,67},{4,68},{5,69},{6,70},{7,71},{8,72},{9,... | collective-permute-start | bytes 983048 | tf_op jit(solution)/shard_map/ppermute | solution.py:45
  81.2 6.7 %collective-permute-start.29 = (bf16[144,1280]{1,0:T(8,128)(2,1)S(1)}, bf16[144,1280]{1,0:T(8,128)(2,1)S(1)}, u32[]{:S(2)}, u32[]{:S(2)}) collective-permute-start(bf16[144,1280]{1,0:T(8,128)(2,1)S(1)} %get-tuple-element.70), channel_id=1, source_target_pairs={{0,192},{1,193},{2,194},{3,195},{4,196},{5,197},{6,198},{7,199},{8... | collective-permute-start | bytes 1105928 | tf_op jit(solution)/shard_map/ppermute | solution.py:45
  85.0 7.6 %collective-permute-start.28 = (bf16[144,1280]{1,0:T(8,128)(2,1)S(1)}, bf16[144,1280]{1,0:T(8,128)(2,1)S(1)}, u32[]{:S(2)}, u32[]{:S(2)}) collective-permute-start(bf16[144,1280]{1,0:T(8,128)(2,1)S(1)} %ring_fold.2), channel_id=1, source_target_pairs={{0,7},{1,0},{2,1},{3,2},{4,3},{5,4},{6,5},{7,6},{8,15},{9,8},{10,9... | collective-permute-start | bytes 1105928 | tf_op jit(solution)/shard_map/ppermute | solution.py:45
  88.0 12.8 %collective-permute-start.35 = (bf16[272,1280]{1,0:T(8,128)(2,1)S(1)}, bf16[272,1280]{1,0:T(8,128)(2,1)S(1)}, u32[]{:S(2)}, u32[]{:S(2)}) collective-permute-start(bf16[272,1280]{1,0:T(8,128)(2,1)S(1)} %get-tuple-element.76), channel_id=1, source_target_pairs={{0,192},{1,193},{2,194},{3,195},{4,196},{5,197},{6,198},{7,199},{8... | collective-permute-start | bytes 2088968 | tf_op jit(solution)/shard_map/ppermute | solution.py:45
  90.2 11.4 %collective-permute-start.36 = (bf16[272,1280]{1,0:T(8,128)(2,1)S(1)}, bf16[272,1280]{1,0:T(8,128)(2,1)S(1)}, u32[]{:S(2)}, u32[]{:S(2)}) collective-permute-start(bf16[272,1280]{1,0:T(8,128)(2,1)S(1)} %get-tuple-element.72), channel_id=1, source_target_pairs={{0,64},{1,65},{2,66},{3,67},{4,68},{5,69},{6,70},{7,71},{8,72},{9,... | collective-permute-start | bytes 2088968 | tf_op jit(solution)/shard_map/ppermute | solution.py:45
  92.7 7.9 %collective-permute-start.31 = (bf16[144,1280]{1,0:T(8,128)(2,1)S(1)}, bf16[144,1280]{1,0:T(8,128)(2,1)S(1)}, u32[]{:S(2)}, u32[]{:S(2)}) collective-permute-start(bf16[144,1280]{1,0:T(8,128)(2,1)S(1)} %ring_fold.3), channel_id=1, source_target_pairs={{0,7},{1,0},{2,1},{3,2},{4,3},{5,4},{6,5},{7,6},{8,15},{9,8},{10,9... | collective-permute-start | bytes 1105928 | tf_op jit(solution)/shard_map/ppermute | solution.py:45
  100.7 5.9 %collective-permute-start.33 = (bf16[80,1280]{1,0:T(8,128)(2,1)S(1)}, bf16[80,1280]{1,0:T(8,128)(2,1)S(1)}, u32[]{:S(2)}, u32[]{:S(2)}) collective-permute-start(bf16[80,1280]{1,0:T(8,128)(2,1)S(1)} %get-tuple-element.75), channel_id=1, source_target_pairs={{0,7},{1,0},{2,1},{3,2},{4,3},{5,4},{6,5},{7,6},{8,15},{9,8},{10,9... | collective-permute-start | bytes 614408 | tf_op jit(solution)/shard_map/ppermute | solution.py:45
  101.8 8.7 %collective-permute-start.37 = (bf16[80,1280]{1,0:T(8,128)(2,1)S(1)}, bf16[80,1280]{1,0:T(8,128)(2,1)S(1)}, u32[]{:S(2)}, u32[]{:S(2)}) collective-permute-start(bf16[80,1280]{1,0:T(8,128)(2,1)S(1)} %get-tuple-element.78), channel_id=1, source_target_pairs={{0,40},{1,41},{2,42},{3,43},{4,44},{5,45},{6,46},{7,47},{8,0},{9,1... | collective-permute-start | bytes 614408 | tf_op jit(solution)/shard_map/ppermute | solution.py:45
  102.2 8.2 %collective-permute-start.38 = (bf16[80,1280]{1,0:T(8,128)(2,1)S(1)}, bf16[80,1280]{1,0:T(8,128)(2,1)S(1)}, u32[]{:S(2)}, u32[]{:S(2)}) collective-permute-start(bf16[80,1280]{1,0:T(8,128)(2,1)S(1)} %get-tuple-element.79), channel_id=1, source_target_pairs={{0,8},{1,9},{2,10},{3,11},{4,12},{5,13},{6,14},{7,15},{8,32},{9,33... | collective-permute-start | bytes 614408 | tf_op jit(solution)/shard_map/ppermute | solution.py:45
  103.4 7.1 %collective-permute-start.39 = (bf16[80,1280]{1,0:T(8,128)(2,1)S(1)}, bf16[80,1280]{1,0:T(8,128)(2,1)S(1)}, u32[]{:S(2)}, u32[]{:S(2)}) collective-permute-start(bf16[80,1280]{1,0:T(8,128)(2,1)S(1)} %get-tuple-element.80), channel_id=1, source_target_pairs={{0,32},{1,33},{2,34},{3,35},{4,36},{5,37},{6,38},{7,39},{8,40},{9,... | collective-permute-start | bytes 614408 | tf_op jit(solution)/shard_map/ppermute | solution.py:45
  106.6 9.5 %collective-permute-start.34 = (bf16[80,1280]{1,0:T(8,128)(2,1)S(1)}, bf16[80,1280]{1,0:T(8,128)(2,1)S(1)}, u32[]{:S(2)}, u32[]{:S(2)}) collective-permute-start(bf16[80,1280]{1,0:T(8,128)(2,1)S(1)} %collective-permute-done.33.refs_3_), channel_id=1, source_target_pairs={{0,16},{1,17},{2,18},{3,19},{4,20},{5,21},{6,22},{7,23},{8,24},{9,... | collective-permute-start | bytes 614408 | tf_op jit(solution)/shard_map/ppermute | solution.py:45
  110.5 5.7 %collective-permute-start.32 = (bf16[64,1280]{1,0:T(8,128)(2,1)S(1)}, bf16[64,1280]{1,0:T(8,128)(2,1)S(1)}, u32[]{:S(2)}, u32[]{:S(2)}) collective-permute-start(bf16[64,1280]{1,0:T(8,128)(2,1)S(1)} %get-tuple-element.74), channel_id=1, source_target_pairs={{0,7},{1,0},{2,1},{3,2},{4,3},{5,4},{6,5},{7,6},{8,15},{9,8},{10,9... | collective-permute-start | bytes 491528 | tf_op jit(solution)/shard_map/ppermute | solution.py:45
